TPU v7x, 32 devices: a whole 2x2x4 slice. The times are simulated.
32 devices in a mesh: row: 4 (over y, core), col: 8 (over z, x).
Axes of the slice: x: 2, y: 2, z: 4, core: 2. Of those that a mesh axis runs over, the one named last changes fastest.
Arguments:
- vectors: float32 [16, 49152], P(None, ('row', 'col')), may hold values from -6 to 6
- tiles: float32 [4, 8, 48, 256, 256], P('row', 'col'), may hold values from -0.375 to 0.375
- tile_rows: int32 [4, 8, 48], P('row', 'col'), may hold values from 0 to 47, as said below
- tile_cols: int32 [4, 8, 48], P('row', 'col'), may hold values from 0 to 23, as said below
- counts: int32 [4, 8], P('row', 'col'), may hold values from 6 to 48, as said below
Outputs:
- residual: float32 [16, 49152], P(None, ('row', 'col'))
- image: float32 [16, 49152], P(None, ('row', 'col'))
- gram: float32 [16, 16], replicated
Inputs may be any that keep to these rules, and one draw needn't show every extreme that they name: Within one cell the slots name distinct tile positions. The live slots of one cell name at most 3 distinct block rows within any one segment (tile_rows // 6 equal), and every cell has a segment with exactly 3. The live slots of one cell name at most 3 distinct block columns within any one segment (tile_cols // 6 equal), and every cell has a segment with exactly 3. `counts`: some cell holds all 48 slots live in every draw; slots at or above a cell's count hold unused tiles.
All inputs are finite; a program needn't handle non-finite values.
Results may differ from a plain program's by a relative error of at most 0.0001.
Values sent between devices are 32-bit elements; how exact they have to be, the bound alone decides.
A program may use at most 64 MiB of HBM per device.

v0:
```python
import jax
import jax.numpy as jnp
from jax import lax
from jax.sharding import PartitionSpec as P

TILE = 256


def local_products(cell_tiles, row_pick, col_pick, row_group, col_group):
    width = row_group.shape[0]
    row_blocks = row_group.reshape(width, row_pick.shape[1], TILE)
    col_blocks = col_group.reshape(width, col_pick.shape[1], TILE)
    from_rows = jnp.einsum("kg,vgj->vkj", row_pick, row_blocks, precision=lax.Precision.HIGHEST)
    from_cols = jnp.einsum("kg,vgj->vkj", col_pick, col_blocks, precision=lax.Precision.HIGHEST)
    to_rows = jnp.einsum("kij,vkj->vki", cell_tiles, from_cols, precision=lax.Precision.HIGHEST)
    to_cols = jnp.einsum("kij,vki->vkj", cell_tiles, from_rows, precision=lax.Precision.HIGHEST)
    row_terms = jnp.einsum("kg,vki->vgi", row_pick, to_rows, precision=lax.Precision.HIGHEST)
    col_terms = jnp.einsum("kg,vkj->vgj", col_pick, to_cols, precision=lax.Precision.HIGHEST)
    return (row_terms, col_terms)


def reduce_rows(row_terms):
    width = row_terms.shape[0]
    return lax.psum_scatter(row_terms.reshape(width, -1), "col", scatter_dimension=1, tiled=True)


def reduce_columns(col_terms):
    width = col_terms.shape[0]
    return lax.psum_scatter(col_terms.reshape(width, -1), "row", scatter_dimension=1, tiled=True)


def apply_whole(block, cell_tiles, row_pick, col_pick):
    row_group = lax.all_gather(block, "col", axis=1, tiled=True)
    col_group = lax.all_gather(block, "row", axis=1, tiled=True)
    row_terms, col_terms = local_products(cell_tiles, row_pick, col_pick, row_group, col_group)
    return reduce_rows(row_terms) + reduce_columns(col_terms)


def apply_hamiltonian(block, cell_tiles, row_pick, col_pick):
    return apply_whole(block, cell_tiles, row_pick, col_pick)


def per_device(vectors, tiles, tile_rows, tile_cols, counts):
    cell_tiles = tiles[0, 0]
    rows = tile_rows[0, 0]
    cols = tile_cols[0, 0]
    segment_blocks = vectors.shape[1] // TILE
    row_span = lax.axis_size("col") * segment_blocks
    col_span = lax.axis_size("row") * segment_blocks
    order_total = vectors.shape[1] * lax.axis_size("row") * lax.axis_size("col")
    alive = (jnp.arange(rows.shape[0], dtype=jnp.int32) < counts[0, 0]).astype(jnp.float32)
    row_pick = (rows[:, None] == jnp.arange(row_span, dtype=jnp.int32)[None, :]).astype(
        jnp.float32
    ) * alive[:, None]
    col_pick = (cols[:, None] == jnp.arange(col_span, dtype=jnp.int32)[None, :]).astype(
        jnp.float32
    ) * alive[:, None]
    product = apply_hamiltonian(vectors, cell_tiles, row_pick, col_pick)
    local_correlation = jnp.einsum("vn,wn->vw", vectors, vectors, precision=lax.Precision.HIGHEST)
    local_projection = jnp.einsum("vn,wn->vw", vectors, product, precision=lax.Precision.HIGHEST)
    correlation, projection = lax.psum((local_correlation, local_projection), ("row", "col"))
    factor = jnp.linalg.cholesky(correlation)
    coeffs = jax.scipy.linalg.cho_solve((factor, True), projection)
    residual = product - jnp.einsum("wv,wn->vn", coeffs, vectors, precision=lax.Precision.HIGHEST)
    image = apply_hamiltonian(residual, cell_tiles, row_pick, col_pick)
    local_gram = jnp.einsum("vn,wn->vw", residual, image, precision=lax.Precision.HIGHEST)
    gram = lax.psum(local_gram, ("row", "col")) / order_total
    return (residual, image, gram)


def solution(mesh):
    in_specs = (
        P(None, ("row", "col")),
        P("row", "col", None, None, None),
        P("row", "col", None),
        P("row", "col", None),
        P("row", "col"),
    )
    out_specs = (P(None, ("row", "col")), P(None, ("row", "col")), P())
    return jax.shard_map(
        per_device, mesh=mesh, in_specs=in_specs, out_specs=out_specs, check_vma=False
    )
```

profile of v0, /device:TPU:0, one launch (start us, length us, event | category | flops | bytes accessed | tf_op | source)
XLA Modules:
  0.0 375.1 jit_solution(17109248143731282500)
XLA Ops:
  7.9 34.0 %all_gather.13 = f32[16,12288]{1,0:T(8,128)S(1)} all-gather(f32[16,1536]{1,0:T(8,128)} %param.5), channel_id=1, replica_groups=mesh['row'=4,'col'=8] {'col'}, dimensions={1}, use_global_device_ids=true | all-gather | bytes 884736 | tf_op jit(solution)/shard_map/all_gather | solution.py:33
  42.2 1.5 convolution_bitcast_fusion.1
  43.7 9.3 %fusion.11 = f32[16,48,256]{2,0,1:T(8,128)S(1)} fusion(f32[1,1,48,256,256]{4,3,2,1,0:T(8,128)} %param.6, f32[16,48,256]{2,1,0:T(8,128)S(1)} %convolution_bitcast_fusion.1), kind=kOutput, calls=%fused_computation.10 | convolution fusion | flops 603979776 | bytes 14155776 | tf_op jit(solution)/shard_map/kij,vki->vkj/dot_general | solution.py:16
  53.1 1.0 fusion.26
  55.0 6.7 %all_gather.12 = f32[16,6144]{1,0:T(8,128)S(1)} all-gather(f32[16,1536]{1,0:T(8,128)S(1)} %copy-done), channel_id=1, replica_groups=mesh['row'=4,'col'=8] {'row'}, dimensions={1}, use_global_device_ids=true | all-gather | bytes 491520 | tf_op jit(solution)/shard_map/all_gather | solution.py:34
  62.6 13.7 %fusion.8 = f32[16,48,256]{2,0,1:T(8,128)S(1)} fusion(f32[1,1,48,256,256]{4,3,2,1,0:T(8,128)} %param.6, f32[16,48,256]{2,1,0:T(8,128)S(1)} %convolution_bitcast_fusion.3), kind=kOutput, calls=%fused_computation.9 | convolution fusion | flops 603979776 | bytes 14155776 | tf_op jit(solution)/shard_map/kij,vkj->vki/dot_general | solution.py:15
  76.3 1.4 fusion.29
  77.7 1.3 copy.30
  79.3 63.3 %reduce-scatter.5.cloned.1.call-done = f32[16,1536]{1,0:T(8,128)} async-done(((f32[16,12288]{1,0:T(8,128)}), f32[16,1536]{1,0:T(8,128)}) %reduce-scatter.5.cloned.1.call-update) | async-done | bytes 98320 | tf_op jit(solution)/shard_map/reduce_scatter | solution.py:24
  142.6 1.0 add.35
  143.8 40.2 %all-reduce = (f32[16,16]{0,1:T(8,128)S(1)}, f32[16,16]{0,1:T(8,128)S(1)}) all-reduce(f32[16,16]{0,1:T(8,128)S(1)} %convolution_bitcast_fusion.4, f32[16,16]{0,1:T(8,128)S(1)} %fusion.86), channel_id=1, replica_groups=mesh['row'=4,'col'=8] {'row','col'}, use_global_device_ids=true, to_apply=%region_5.6 | all-reduce | flops 512 | bytes 4096 | tf_op jit(solution)/shard_map/psum | solution.py:61
  184.0 1.5 cholesky.16
  186.8 1.2 custom-call.10
  188.7 7.3 %all_gather.14 = f32[16,6144]{1,0:T(8,128)S(1)} all-gather(f32[16,1536]{1,0:T(8,128)S(1)} %convolution_subtract_fusion), channel_id=1, replica_groups=mesh['row'=4,'col'=8] {'row'}, dimensions={1}, use_global_device_ids=true | all-gather | bytes 491520 | tf_op jit(solution)/shard_map/all_gather | solution.py:34
  196.0 32.3 %all_gather.15 = f32[16,12288]{1,0:T(8,128)S(1)} all-gather(f32[16,1536]{1,0:T(8,128)S(1)} %convolution_subtract_fusion), channel_id=1, replica_groups=mesh['row'=4,'col'=8] {'col'}, dimensions={1}, use_global_device_ids=true | all-gather | bytes 884736 | tf_op jit(solution)/shard_map/all_gather | solution.py:33
  230.3 9.3 %fusion.17 = f32[16,48,256]{2,0,1:T(8,128)S(1)} fusion(f32[1,1,48,256,256]{4,3,2,1,0:T(8,128)} %param.6, f32[16,48,256]{2,1,0:T(8,128)S(1)} %convolution_bitcast_fusion), kind=kOutput, calls=%fused_computation.12 | convolution fusion | flops 603979776 | bytes 14155776 | tf_op jit(solution)/shard_map/kij,vki->vkj/dot_general | solution.py:16
  239.6 1.0 fusion.20
  241.8 13.5 %fusion.14 = f32[16,48,256]{2,0,1:T(8,128)S(1)} fusion(f32[1,1,48,256,256]{4,3,2,1,0:T(8,128)} %param.6, f32[16,48,256]{2,1,0:T(8,128)S(1)} %convolution_bitcast_fusion.2), kind=kOutput, calls=%fused_computation.11 | convolution fusion | flops 603979776 | bytes 14155776 | tf_op jit(solution)/shard_map/kij,vkj->vki/dot_general | solution.py:15
  255.4 1.4 fusion.23
  256.8 1.3 copy.34
  258.1 2.8 reduce-scatter.11.cloned.1.call-done
  260.9 65.9 %reduce-scatter.9.cloned.1.call-done = f32[16,1536]{1,0:T(8,128)} async-done(((f32[16,12288]{1,0:T(8,128)}), f32[16,1536]{1,0:T(8,128)}) %reduce-scatter.9.cloned.1.call-update) | async-done | bytes 98320 | tf_op jit(solution)/shard_map/reduce_scatter | solution.py:24
  326.8 1.0 add.37
  328.0 40.0 %psum.23 = f32[16,16]{1,0:T(8,128)S(1)} all-reduce(f32[16,16]{1,0:T(8,128)S(1)} %fusion.87), channel_id=1, replica_groups=mesh['row'=4,'col'=8] {'row','col'}, use_global_device_ids=true, to_apply=%region_8.9 | all-reduce | flops 256 | bytes 2048 | tf_op jit(solution)/shard_map/psum | solution.py:67
  (41 shorter events, 8.7 us)
Async XLA Ops:
  7.2 47.8 %copy-start = (f32[16,1536]{1,0:T(8,128)S(1)}, f32[16,1536]{1,0:T(8,128)}, u32[]{:S(2)}) copy-start(f32[16,1536]{1,0:T(8,128)} %param.5) | copy-start | bytes 294916
  7.2 45.9 %copy-start.3 = (s32[1,1,48]{2,1,0:T(1,128)S(1)}, s32[1,1,48]{2,1,0:T(1,128)}, u32[]{:S(2)}) copy-start(s32[1,1,48]{2,1,0:T(1,128)} %param.8) | copy-start | bytes 580
  7.2 72.1 %reduce-scatter.7.cloned.1.call-start = ((), (), s32[]{:S(2)}) async-start(), calls=%async_computation.5 | async-start | bytes 491520 | tf_op jit(solution)/shard_map/reduce_scatter | solution.py:29
  53.0 23.3 %copy-start.4 = (s32[1,1,48]{2,1,0:T(1,128)S(1)}, s32[1,1,48]{2,1,0:T(1,128)}, u32[]{:S(2)}) copy-start(s32[1,1,48]{2,1,0:T(1,128)} %param.7) | copy-start | bytes 580
  55.0 87.7 %reduce-scatter.5.cloned.1.call-start = ((), (), s32[]{:S(2)}) async-start(), calls=%async_computation.4 | async-start | bytes 884736 | tf_op jit(solution)/shard_map/reduce_scatter | solution.py:24
  79.1 181.8 %reduce-scatter.11.cloned.1.call-start = ((), (), s32[]{:S(2)}) async-start(), calls=%async_computation.7 | async-start | bytes 491520 | tf_op jit(solution)/shard_map/reduce_scatter | solution.py:29
  188.7 139.1 %copy-start.1 = (f32[16,1536]{1,0:T(8,128)}, f32[16,1536]{1,0:T(8,128)S(1)}, u32[]{:S(2)}) copy-start(f32[16,1536]{1,0:T(8,128)S(1)} %convolution_subtract_fusion) | copy-start | bytes 294916
  241.5 85.3 %reduce-scatter.9.cloned.1.call-start = ((), (), s32[]{:S(2)}) async-start(), calls=%async_computation.6 | async-start | bytes 884736 | tf_op jit(solution)/shard_map/reduce_scatter | solution.py:24
  327.8 40.8 %copy-start.2 = (f32[16,1536]{1,0:T(8,128)}, f32[16,1536]{1,0:T(8,128)S(1)}, u32[]{:S(2)}) copy-start(f32[16,1536]{1,0:T(8,128)S(1)} %add.37) | copy-start | bytes 294916
Sparse Core Ops, SparseCore 0:
  55.1 21.7 reduce-scatter.6
  80.2 62.3 reduce-scatter.4
  241.7 19.1 reduce-scatter.10
  264.4 62.3 reduce-scatter.8
where the time goes:
time: 376 us; the launch traced here: 375 us
  blocking collectives  160 us (43%)
  waiting for transfers between devices  132 us (35%)
  matrix products  55.8 us (15%)
  between operations  14.6 us (4%)
  other arithmetic  6.52 us (2%)
  local copies, waits for them, and re-layouts  5.22 us (1%)
    reduce_scatter x2, waiting for transfers between devices, reduce_rows(): lax.psum_scatter(row_terms.reshape(width, -1), 'col', scatter_dimension=1...  129 us
    all_gather x2, blocking collectives, apply_whole(): row_group = lax.all_gather(block, 'col', axis=1, tiled=True)  66.3 us
    psum x1, blocking collectives, per_device(): lax.psum((local_correlation, local_projection), ('row', 'col'))  40.2 us
    psum x1, blocking collectives, per_device(): gram = lax.psum(local_gram, ('row', 'col')) / order_total  40 us
    dot_general x2, matrix products, local_products(): jnp.einsum('kij,vkj->vki', cell_tiles, from_cols, precision=lax.Precision...  27.2 us
    dot_general x2, matrix products, local_products(): jnp.einsum('kij,vki->vkj', cell_tiles, from_rows, precision=lax.Precision...  18.7 us
    all_gather x2, blocking collectives, apply_whole(): col_group = lax.all_gather(block, 'row', axis=1, tiled=True)  13.9 us
  transfers between devices with their start and end apart: 4, of which 3 were waited for; matrix products, arithmetic and copies ran while one was open for 9% of the time, Pallas kernels for 0%

commit v1 on v0

v1 whole, which is shorter than its diff:
```python
import functools

import jax
import jax.numpy as jnp
from jax import lax
from jax.experimental import pallas as pl
from jax.experimental.pallas import tpu as pltpu
from jax.sharding import PartitionSpec as P

TILE = 256
CAP = 3
POS = 8
MESH = pl.DeviceIdType.MESH
F32 = jnp.float32
BF16 = jnp.bfloat16
EXACT = lax.Precision.HIGHEST


def dot_nt(a, b, precision=None):
    return lax.dot_general(
        a, b, (((1,), (1,)), ((), ())), precision=precision, preferred_element_type=F32
    )


def dot_nn(a, b, precision=None):
    return lax.dot_general(
        a, b, (((1,), (0,)), ((), ())), precision=precision, preferred_element_type=F32
    )


def split(x):
    high = x.astype(BF16)
    return high, (x - high.astype(F32)).astype(BF16)


def prep_kernel(n_row, n_col, segb, rows, cols, count, out):
    slots = rows.shape[2]
    live_count = count[0, 0]

    def clear(i, carry):
        for lane in range(POS + segb):
            out[i, 0, lane] = 0
        return carry

    lax.fori_loop(0, n_row + n_col, clear, 0)

    def touch(k, carry):
        live = (k < live_count).astype(jnp.int32)
        for ids, base in ((rows, 0), (cols, n_col)):
            which = ids[0, 0, k]
            seg = base + which // segb
            lane = POS + which % segb
            out[seg, 0, lane] = jnp.maximum(out[seg, 0, lane], live)
        return carry

    lax.fori_loop(0, slots, touch, 0)

    def rank(i, carry):
        n = 0
        for b in range(segb):
            named = out[i, 0, POS + b] > 0
            out[i, 0, POS + b] = jnp.where(named, n, CAP)
            out[i, 0, jnp.where(named, n, POS - 1)] = b
            n = n + named.astype(jnp.int32)
        return carry

    lax.fori_loop(0, n_row + n_col, rank, 0)

    def place(k, carry):
        for line, ids, base in ((n_row + n_col, rows, 0), (n_row + n_col + 1, cols, n_col)):
            which = ids[0, 0, k]
            seg = which // segb
            at = seg * CAP + out[base + seg, 0, POS + which % segb]
            out[line, 0, k] = jnp.where(k < live_count, at, -1)
        return carry

    lax.fori_loop(0, slots, place, 0)


def main_kernel(n_row, n_col, segb, order, *refs):
    (tab_s, tab_v, vec, tiles, residual, image, gram) = refs[:7]
    (
        raw, tile_hi, tile_lo, pick_r, pick_c, z_hi, z_lo, idx_v, idx_s, own,
        zr, zc, corr_1, corr_2, gram_1, gram_2, tile_sem, idx_sem,
    ) = refs[7:25]
    rounds = [refs[25:38], refs[38:51]]
    (ir_s, ir_r, ic_s, ic_r, c1_s, c1_r, c2_s, c2_r, g1_s, g1_r, g2_s, g2_r) = refs[51:63]
    nv = vec.shape[0]
    slots = raw.shape[0]
    row = lax.axis_index("row")
    col = lax.axis_index("col")
    axes = {
        "row": (n_row, row, lambda p: (p, col)),
        "col": (n_col, col, lambda p: (row, p)),
    }

    def each_peer(axis, body):
        n, me, device = axes[axis]

        def step(d, carry):
            body(lax.rem(me + d, n))
            return carry

        lax.fori_loop(1, n, step, 0)

    def copy(axis, source, target, send, recv, p, slot):
        return pltpu.make_async_remote_copy(
            src_ref=source, dst_ref=target, send_sem=send.at[p], recv_sem=recv.at[slot],
            device_id=axes[axis][2](p), device_id_type=MESH,
        )

    class Exchange:
        def __init__(self, axis, source, target, send, recv):
            self.axis, self.source, self.target = axis, source, target
            self.send, self.recv = send, recv

        def make(self, p, slot):
            return copy(self.axis, self.source(p), self.target(slot), self.send, self.recv, p, slot)

        def start(self):
            me = axes[self.axis][1]
            each_peer(self.axis, lambda p: self.make(p, me).start())

        def wait_recv(self):
            each_peer(self.axis, lambda p: self.make(p, p).wait_recv())

        def wait_send(self):
            me = axes[self.axis][1]
            each_peer(self.axis, lambda p: self.make(p, me).wait_send())

    chunk = 8 if slots % 8 == 0 else 1
    n_chunks = slots // chunk
    tile_copies = [
        pltpu.make_async_copy(
            tiles.at[0, 0, pl.ds(i * chunk, chunk)], raw.at[pl.ds(i * chunk, chunk)], tile_sem.at[i]
        )
        for i in range(n_chunks)
    ]
    for c in tile_copies:
        c.start()

    barrier = pltpu.get_barrier_semaphore()
    for axis in ("row", "col"):
        device = axes[axis][2]
        each_peer(
            axis,
            lambda p: pl.semaphore_signal(
                barrier, inc=1, device_id=device(p), device_id_type=MESH
            ),
        )
    idx_v[col] = tab_v[col]
    idx_v[n_col + row] = tab_v[n_col + row]
    corr_1[...] = jnp.zeros_like(corr_1)
    corr_2[...] = jnp.zeros_like(corr_2)
    gram_1[...] = jnp.zeros_like(gram_1)
    gram_2[...] = jnp.zeros_like(gram_2)
    zero_block = jnp.zeros((nv, TILE), F32)
    for r in rounds:
        back_r, back_c = r[4], r[5]
        for i in range(n_col):
            back_r[i, CAP] = zero_block
        for i in range(n_row):
            back_c[i, CAP] = zero_block
    pl.semaphore_wait(barrier, n_row + n_col - 2)

    idx_r = Exchange("col", lambda p: tab_v.at[p], lambda i: idx_v.at[i], ir_s, ir_r)
    idx_c = Exchange("row", lambda p: tab_v.at[n_col + p], lambda i: idx_v.at[n_col + i], ic_s, ic_r)
    idx_r.start()
    idx_c.start()
    for b in range(segb):
        own[0, b] = vec[:, b * TILE:(b + 1) * TILE]
    idx_c.wait_recv()
    idx_r.wait_recv()
    to_smem = pltpu.make_async_copy(idx_v, idx_s, idx_sem)
    to_smem.start()
    to_smem.wait()

    def build_pick(line, pick):
        n, wide = pick.shape
        lane = lax.broadcasted_iota(jnp.int32, (8, wide), 1)
        slot_of, vector_of = lane // nv, lane % nv

        def step(k, carry):
            return jnp.where(slot_of == k, vector_of + nv * tab_s[line, 0, k], carry)

        wanted = lax.fori_loop(0, slots, step, jnp.full((8, wide), -1, jnp.int32))[0:1]
        part = CAP * nv

        def fill(i, carry):
            at = lax.broadcasted_iota(jnp.int32, (part, wide), 0) + i * part
            pick[pl.ds(pl.multiple_of(i * part, part), part), :] = jnp.where(
                at == wanted, 1.0, 0.0
            ).astype(BF16)
            return carry

        lax.fori_loop(0, n // part, fill, 0)

    def split_tiles():
        for i in range(n_chunks):
            tile_copies[i].wait()

            def step(k, carry):
                high, low = split(raw[k])
                tile_hi[k] = high
                tile_lo[k] = low
                return carry

            lax.fori_loop(i * chunk, (i + 1) * chunk, step, 0)

    def split_blocks(n, source, target):
        def step(i, carry):
            for j in range(CAP):
                high, low = split(source[i, j])
                target[i * CAP + j, 0:nv] = high
                target[i * CAP + j, nv:2 * nv] = low
            return carry

        lax.fori_loop(0, n, step, 0)

    def multiply(line, blocks, pick, n, out, dot):
        width = 4 if slots % 4 == 0 else 1

        def step(g, carry):
            for u in range(width):
                k = g * width + u
                x = blocks[jnp.maximum(tab_s[line, 0, k], 0)]
                wide = dot(x, tile_hi[k])
                z = wide[0:nv] + wide[nv:2 * nv] + dot(x[0:nv], tile_lo[k])
                high, low = split(z)
                z_hi[k] = high
                z_lo[k] = low
            return carry

        lax.fori_loop(0, slots // width, step, 0)
        flat = (slots * nv, TILE)
        y = dot_nn(pick[...], z_hi[...].reshape(flat)) + dot_nn(pick[...], z_lo[...].reshape(flat))
        out[...] = y.reshape(n, CAP, nv, TILE)

    exchanges = [idx_r, idx_c]

    def apply(which, first, after_rows, after_gather, after_columns):
        send_r, send_c, got_r, got_c, back_r, back_c, y_r, y_c = rounds[which][:8]
        gr_s, gc_s, br_s, bc_s, rr = rounds[which][8:]
        gather_r = Exchange("col", lambda p: send_r.at[p], lambda i: got_r.at[i], gr_s, rr.at[0])
        gather_c = Exchange("row", lambda p: send_c.at[p], lambda i: got_c.at[i], gc_s, rr.at[1])
        scatter_r = Exchange("col", lambda p: y_r.at[p], lambda i: back_r.at[i, pl.ds(0, CAP)], br_s, rr.at[2])
        scatter_c = Exchange("row", lambda p: y_c.at[p], lambda i: back_c.at[i, pl.ds(0, CAP)], bc_s, rr.at[3])
        exchanges.extend([gather_r, gather_c, scatter_r, scatter_c])

        def pack(axis, base, exchange, send, got):
            n, me, device = axes[axis]

            def one(p):
                for j in range(CAP):
                    send[p, j] = own[which, idx_s[base + p, 0, j]]
                exchange.make(p, me).start()

            each_peer(axis, one)
            for j in range(CAP):
                got[me, j] = own[which, idx_s[base + me, 0, j]]

        pack("row", n_col, gather_c, send_c, got_c)
        pack("col", 0, gather_r, send_r, got_r)
        first()
        gather_c.wait_recv()
        split_blocks(n_row, got_c, zc)
        multiply(n_row + n_col + 1, zc, pick_r, n_col, y_r, dot_nt)
        scatter_r.start()
        for j in range(CAP):
            back_r[col, j] = y_r[col, j]
        after_rows()
        gather_r.wait_recv()
        split_blocks(n_col, got_r, zr)
        after_gather(got_r, y_r)
        multiply(n_row + n_col, zr, pick_c, n_row, y_c, dot_nn)
        scatter_c.start()
        for j in range(CAP):
            back_c[row, j] = y_c[row, j]
        after_columns()
        scatter_c.wait_recv()
        scatter_r.wait_recv()
        for b in range(segb):
            total = zero_block
            for i in range(n_row):
                total = total + back_c[i, idx_s[n_col + i, 0, POS + b]]
            for i in range(n_col):
                total = total + back_r[i, idx_s[i, 0, POS + b]]
            own[which + 1, b] = total

    def setup():
        build_pick(n_row + n_col, pick_r)
        build_pick(n_row + n_col + 1, pick_c)
        split_tiles()

    nothing = lambda *unused: None
    apply(0, setup, nothing, nothing, nothing)

    corr_row = Exchange("row", lambda p: corr_1.at[row], lambda i: corr_1.at[i], c1_s, c1_r)
    corr_col = Exchange("col", lambda p: corr_2.at[col], lambda i: corr_2.at[i], c2_s, c2_r)
    gram_row = Exchange("row", lambda p: gram_1.at[row], lambda i: gram_1.at[i], g1_s, g1_r)
    gram_col = Exchange("col", lambda p: gram_2.at[col], lambda i: gram_2.at[i], g2_s, g2_r)
    exchanges.extend([corr_row, corr_col, gram_row, gram_col])

    def total_of(ref, n):
        total = ref[0]
        for i in range(1, n):
            total = total + ref[i]
        return total

    def correlate():
        total = jnp.zeros((2 * nv, 2 * nv), F32)
        for b in range(segb):
            both = jnp.concatenate([own[0, b], own[1, b]], axis=0)
            total = total + dot_nt(both, both, EXACT)
        corr_1[row, :, 0:2 * nv] = total
        corr_row.start()

    def correlate_on():
        corr_row.wait_recv()
        corr_2[col] = total_of(corr_1, n_row)
        corr_col.start()

    def gram_terms(got_r, y_r):
        def step(i, total):
            for j in range(CAP):
                total = total + dot_nt(got_r[i, j], y_r[i, j], EXACT)
            return total

        gram_1[row, :, 0:nv] = lax.fori_loop(0, n_col, step, jnp.zeros((nv, nv), F32))
        gram_row.start()

    answers = []

    def solve():
        gram_row.wait_recv()
        gram_2[col] = total_of(gram_1, n_row)
        gram_col.start()
        corr_col.wait_recv()
        sums = total_of(corr_2, n_col)
        lanes = sums.shape[1]
        m = sums[0:nv]
        line = lax.broadcasted_iota(jnp.int32, (nv, lanes), 0)
        lane = lax.broadcasted_iota(jnp.int32, (nv, lanes), 1)
        for i in range(nv):
            pivot_row = m[i:i + 1, :] / m[i:i + 1, i:i + 1]
            m = jnp.where(line == i, pivot_row, m - m[:, i:i + 1] * pivot_row)
        second = jnp.where(lane == line + nv, 1.0, 0.0).astype(F32)
        coeffs_t = dot_nt(second, m, EXACT)
        proj = dot_nt(sums[0:nv], second, EXACT)
        squares = dot_nt(sums[nv:2 * nv], second, EXACT)
        answers.extend([coeffs_t, proj, squares])
        for b in range(segb):
            residual[:, b * TILE:(b + 1) * TILE] = own[1, b] - dot_nn(coeffs_t, own[0, b], EXACT)

    apply(1, correlate, correlate_on, gram_terms, solve)
    coeffs_t, proj, squares = answers
    for b in range(segb):
        image[:, b * TILE:(b + 1) * TILE] = own[2, b] - dot_nn(coeffs_t, own[1, b], EXACT)
    gram_col.wait_recv()
    half = total_of(gram_2, n_col)[:, 0:nv]
    eye = jnp.where(
        lax.broadcasted_iota(jnp.int32, (nv, nv), 0) == lax.broadcasted_iota(jnp.int32, (nv, nv), 1),
        1.0, 0.0,
    ).astype(F32)
    whole = half + dot_nt(eye, half, EXACT)
    whole = whole - dot_nn(coeffs_t, squares, EXACT) - dot_nt(squares, coeffs_t, EXACT)
    whole = whole + dot_nt(dot_nn(coeffs_t, proj, EXACT), coeffs_t, EXACT)
    gram[...] = whole / order
    for e in exchanges:
        e.wait_send()


def per_device(n_row, n_col, vectors, tiles, tile_rows, tile_cols, counts):
    nv, width = vectors.shape
    segb = width // TILE
    slots = tiles.shape[2]
    lines = n_row + n_col + 2
    smem = pl.BlockSpec(memory_space=pltpu.SMEM)
    vmem = pl.BlockSpec(memory_space=pltpu.VMEM)
    table = pl.pallas_call(
        functools.partial(prep_kernel, n_row, n_col, segb),
        out_shape=jax.ShapeDtypeStruct((lines, 1, 128), jnp.int32),
        in_specs=[smem] * 3,
        out_specs=smem,
    )(tile_rows, tile_cols, counts)
    dma = pltpu.SemaphoreType.DMA
    rb, cb = (n_col, CAP, nv, TILE), (n_row, CAP, nv, TILE)
    most = max(n_row, n_col)
    one_round = [
        pltpu.VMEM(rb, F32), pltpu.VMEM(cb, F32), pltpu.VMEM(rb, F32), pltpu.VMEM(cb, F32),
        pltpu.VMEM((n_col, CAP + 1, nv, TILE), F32), pltpu.VMEM((n_row, CAP + 1, nv, TILE), F32),
        pltpu.VMEM(rb, F32), pltpu.VMEM(cb, F32),
        dma((n_col,)), dma((n_row,)), dma((n_col,)), dma((n_row,)), dma((4, most)),
    ]
    scratch = [
        pltpu.VMEM((slots, TILE, TILE), F32),
        pltpu.VMEM((slots, TILE, TILE), BF16),
        pltpu.VMEM((slots, TILE, TILE), BF16),
        pltpu.VMEM((n_col * CAP * nv, slots * nv), BF16),
        pltpu.VMEM((n_row * CAP * nv, slots * nv), BF16),
        pltpu.VMEM((slots, nv, TILE), BF16),
        pltpu.VMEM((slots, nv, TILE), BF16),
        pltpu.VMEM((n_row + n_col, 1, 128), jnp.int32),
        pltpu.SMEM((n_row + n_col, 1, 128), jnp.int32),
        pltpu.VMEM((3, segb, nv, TILE), F32),
        pltpu.VMEM((n_col * CAP, 2 * nv, TILE), BF16),
        pltpu.VMEM((n_row * CAP, 2 * nv, TILE), BF16),
        pltpu.VMEM((n_row, 2 * nv, 128), F32),
        pltpu.VMEM((n_col, 2 * nv, 128), F32),
        pltpu.VMEM((n_row, nv, 128), F32),
        pltpu.VMEM((n_col, nv, 128), F32),
        dma((slots,)),
        dma(()),
        *one_round,
        *one_round,
        dma((n_col,)), dma((n_col,)), dma((n_row,)), dma((n_row,)),
        dma((n_row,)), dma((n_row,)), dma((n_col,)), dma((n_col,)),
        dma((n_row,)), dma((n_row,)), dma((n_col,)), dma((n_col,)),
    ]
    order = width * n_row * n_col
    return pl.pallas_call(
        functools.partial(main_kernel, n_row, n_col, segb, order),
        out_shape=(
            jax.ShapeDtypeStruct((nv, width), F32),
            jax.ShapeDtypeStruct((nv, width), F32),
            jax.ShapeDtypeStruct((nv, nv), F32),
        ),
        in_specs=[smem, vmem, vmem, pl.BlockSpec(memory_space=pl.ANY)],
        out_specs=(vmem, vmem, vmem),
        scratch_shapes=scratch,
        compiler_params=pltpu.CompilerParams(
            collective_id=0, has_side_effects=True, vmem_limit_bytes=52 * 2**20
        ),
    )(table, table, vectors, tiles)


def solution(mesh):
    in_specs = (
        P(None, ("row", "col")),
        P("row", "col", None, None, None),
        P("row", "col", None),
        P("row", "col", None),
        P("row", "col"),
    )
    out_specs = (P(None, ("row", "col")), P(None, ("row", "col")), P())
    body = functools.partial(per_device, mesh.shape["row"], mesh.shape["col"])
    return jax.shard_map(body, mesh=mesh, in_specs=in_specs, out_specs=out_specs, check_vma=False)
```

time: 376 us -> 66.5 us (0.18)
  blocking collectives: 160 us -> 0 us
  waiting for transfers between devices: 132 us -> 0 us
  Pallas kernels: 0 us -> 61.5 us
  matrix products: 55.8 us -> 0 us
  between operations: 14.6 us -> 1.3 us
  other arithmetic: 6.52 us -> 0 us
    reduce_scatter x4 -> x0, waiting for transfers between devices: 132 us -> none  [the longest x2 129 us: reduce_rows(): lax.psum_scatter(row_terms.reshape(width, -1), 'col', scatter_dimension=1...]
    all_gather x4 -> x0, blocking collectives: 80.3 us -> none  [the longest x2 66.3 us: apply_whole(): row_group = lax.all_gather(block, 'col', axis=1, tiled=True)]
    psum x2 -> x0, blocking collectives: 80.2 us -> none  [the longest x1 40.2 us: per_device(): lax.psum((local_correlation, local_projection), ('row', 'col'))]
    pallas_call x0 -> x2, Pallas kernels: none -> 61.5 us  [the longest x1 56.9 us: per_device(): pl.pallas_call(functools.partial(main_kernel, n_row, n_col, segb, order),...]
    dot_general x16 -> x0, matrix products: 55.5 us -> none  [the longest x2 27.2 us: local_products(): jnp.einsum('kij,vkj->vki', cell_tiles, from_cols, precision=lax.Precision...]
    another operation x5 -> x0, other arithmetic: 4.01 us -> none  [the longest x3 2.13 us: per_device(): factor = jnp.linalg.cholesky(correlation)]
  transfers between devices with their start and end apart: 4 -> 0, of which waited for: 3 -> 0; matrix products, arithmetic and copies ran while one was open for 9% -> 0% of each run, Pallas kernels for 0% -> 0%
where the time goes in v1:
time: 66.5 us; the launch traced here: 66.3 us
  Pallas kernels  61.5 us (92%)
  local copies, waits for them, and re-layouts  3.46 us (5%)
  between operations  1.3 us (2%)
    pallas_call x1, Pallas kernels, per_device(): pl.pallas_call(functools.partial(main_kernel, n_row, n_col, segb, order),...  56.9 us
    pallas_call x1, Pallas kernels, per_device(): pl.pallas_call(functools.partial(prep_kernel, n_row, n_col, segb), out_sh...  4.57 us
    unnamed x7, local copies, waits for them, and re-layouts  3.46 us

profile of v1, /device:TPU:0, one launch (start us, length us, event | category | flops | bytes accessed | tf_op | source)
XLA Modules:
  0.0 66.3 jit_solution(2979823709237247865)
XLA Ops:
  1.3 4.6 %shard_map.76.refs_0_.refs_1_ = s32[14,1,128]{2,1,0:T(1,128)} custom-call(s32[1,1,48]{2,1,0:T(1,128)} %rows.1, s32[1,1,48]{2,1,0:T(1,128)} %cols.1, s32[1,1]{1,0:T(1,128)S(6)} %copy.11.count), custom_call_target="tpu_custom_call" | custom-call | tf_op jit(solution)/shard_map/pallas_call | solution.py:380
  5.9 0.0 copy-start
  5.9 0.9 %copy-done = f32[16,1536]{1,0:T(8,128)S(1)} copy-done((f32[16,1536]{1,0:T(8,128)S(1)}, f32[16,1536]{1,0:T(8,128)}, u32[]{:S(2)}) %copy-start) | copy-done | bytes 98328
  6.8 0.0 copy-start.1
  6.8 0.7 %copy-done.1 = s32[14,1,128]{2,1,0:T(1,128)S(1)} copy-done((s32[14,1,128]{2,1,0:T(1,128)S(1)}, s32[14,1,128]{2,1,0:T(1,128)}, u32[]{:S(2)}) %copy-start.1) | copy-done | bytes 7192
  7.4 56.9 %shard_map.77 = (f32[16,1536]{1,0:T(8,128)S(1)}, f32[16,1536]{1,0:T(8,128)S(1)}, f32[16,16]{1,0:T(8,128)S(1)}) custom-call(s32[14,1,128]{2,1,0:T(1,128)S(1)} %copy-done.1, s32[14,1,128]{2,1,0:T(1,128)S(1)} %copy-done.1, f32[16,1536]{1,0:T(8,128)S(1)} %copy-done, f32[1,1,48,256,256]{4,3,2,1,0:T(8,128)} %refs_3_.1), custom_call_target="tpu_custom_call" | custom-call | tf_op jit(solution)/shard_map/pallas_call | solution.py:421
  64.4 0.6 copy.12
  65.0 0.6 copy.13
  65.7 0.6 copy.14
Async XLA Ops:
  5.9 0.9 %copy-start = (f32[16,1536]{1,0:T(8,128)S(1)}, f32[16,1536]{1,0:T(8,128)}, u32[]{:S(2)}) copy-start(f32[16,1536]{1,0:T(8,128)} %refs_2_.1) | copy-start | bytes 294916
  6.8 0.7 %copy-start.1 = (s32[14,1,128]{2,1,0:T(1,128)S(1)}, s32[14,1,128]{2,1,0:T(1,128)}, u32[]{:S(2)}) copy-start(s32[14,1,128]{2,1,0:T(1,128)} %shard_map.76.refs_0_.refs_1_) | copy-start | bytes 21508

commit v2 on v1

--- a/solution.py
+++ b/solution.py
@@ -9,7 +9,7 @@
 
 TILE = 256
 CAP = 3
-POS = 8
+NEED = 8
 MESH = pl.DeviceIdType.MESH
 F32 = jnp.float32
 BF16 = jnp.bfloat16
@@ -33,58 +33,16 @@
     return high, (x - high.astype(F32)).astype(BF16)
 
 
-def prep_kernel(n_row, n_col, segb, rows, cols, count, out):
-    slots = rows.shape[2]
-    live_count = count[0, 0]
-
-    def clear(i, carry):
-        for lane in range(POS + segb):
-            out[i, 0, lane] = 0
-        return carry
-
-    lax.fori_loop(0, n_row + n_col, clear, 0)
-
-    def touch(k, carry):
-        live = (k < live_count).astype(jnp.int32)
-        for ids, base in ((rows, 0), (cols, n_col)):
-            which = ids[0, 0, k]
-            seg = base + which // segb
-            lane = POS + which % segb
-            out[seg, 0, lane] = jnp.maximum(out[seg, 0, lane], live)
-        return carry
-
-    lax.fori_loop(0, slots, touch, 0)
-
-    def rank(i, carry):
-        n = 0
-        for b in range(segb):
-            named = out[i, 0, POS + b] > 0
-            out[i, 0, POS + b] = jnp.where(named, n, CAP)
-            out[i, 0, jnp.where(named, n, POS - 1)] = b
-            n = n + named.astype(jnp.int32)
-        return carry
-
-    lax.fori_loop(0, n_row + n_col, rank, 0)
-
-    def place(k, carry):
-        for line, ids, base in ((n_row + n_col, rows, 0), (n_row + n_col + 1, cols, n_col)):
-            which = ids[0, 0, k]
-            seg = which // segb
-            at = seg * CAP + out[base + seg, 0, POS + which % segb]
-            out[line, 0, k] = jnp.where(k < live_count, at, -1)
-        return carry
-
-    lax.fori_loop(0, slots, place, 0)
-
-
 def main_kernel(n_row, n_col, segb, order, *refs):
-    (tab_s, tab_v, vec, tiles, residual, image, gram) = refs[:7]
+    (rows, cols, count, vec, tiles, residual, image, gram) = refs[:8]
+    refs = refs[8:]
     (
         raw, tile_hi, tile_lo, pick_r, pick_c, z_hi, z_lo, idx_v, idx_s, own,
-        zr, zc, corr_1, corr_2, gram_1, gram_2, tile_sem, idx_sem,
-    ) = refs[7:25]
-    rounds = [refs[25:38], refs[38:51]]
-    (ir_s, ir_r, ic_s, ic_r, c1_s, c1_r, c2_s, c2_r, g1_s, g1_r, g2_s, g2_r) = refs[51:63]
+        zr, zc, corr_1, corr_2, gram_1, gram_2, tab_v, tab_s, slot_s, out_v, later, small,
+        tile_sem, idx_sem, tab_sem, vec_sem, out_sem,
+    ) = refs[:27]
+    rounds = [refs[27:40], refs[40:53]]
+    (ir_s, ir_r, ic_s, ic_r, c1_s, c1_r, c2_s, c2_r, g1_s, g1_r, g2_s, g2_r) = refs[53:65]
     nv = vec.shape[0]
     slots = raw.shape[0]
     row = lax.axis_index("row")
@@ -136,7 +94,11 @@
         )
         for i in range(n_chunks)
     ]
-    for c in tile_copies:
+    vec_copies = [
+        pltpu.make_async_copy(vec.at[:, pl.ds(b * TILE, TILE)], own.at[0, b], vec_sem.at[b])
+        for b in range(segb)
+    ]
+    for c in vec_copies + tile_copies:
         c.start()
 
     barrier = pltpu.get_barrier_semaphore()
@@ -148,8 +110,44 @@
                 barrier, inc=1, device_id=device(p), device_id_type=MESH
             ),
         )
-    idx_v[col] = tab_v[col]
-    idx_v[n_col + row] = tab_v[n_col + row]
+
+    lane = lax.broadcasted_iota(jnp.int32, (8, 128), 1)
+    line = lax.broadcasted_iota(jnp.int32, (8, 128), 0)
+    live_count = count[0, 0]
+    seg = jnp.zeros((8, 128), jnp.int32)
+    for i in range(1, 128 // segb + 1):
+        seg = seg + (lane >= i * segb).astype(jnp.int32)
+    block = lane - seg * segb
+
+    def touch(g, named):
+        for u in range(unroll):
+            k = g * unroll + u
+            live = k < live_count
+            which = jnp.where(
+                line == 0, jnp.where(live, rows[0, 0, k], -1), jnp.where(live, cols[0, 0, k], -1)
+            )
+            named = jnp.where(lane == which, 1, named)
+        return named
+
+    unroll = 8 if slots % 8 == 0 else 1
+    named = lax.fori_loop(0, slots // unroll, touch, jnp.zeros((8, 128), jnp.int32))
+    rank = jnp.zeros((8, 128), jnp.int32)
+    for d in range(1, segb):
+        rank = rank + jnp.where(block >= d, pltpu.roll(named, d, 1), 0)
+    need = jnp.zeros((8, 128), jnp.int32)
+    for d in range(segb):
+        moved = jnp.where((named > 0) & (block - rank == d), block, 0)
+        need = need + (pltpu.roll(moved, 128 - d, 1) if d else moved)
+    message = jnp.where(named > 0, rank, CAP) + NEED * need
+    place = seg * CAP + rank
+    tab_v[0] = message[0:1]
+    tab_v[1] = message[1:2]
+    tab_v[2] = place[0:1]
+    tab_v[3] = place[1:2]
+    idx_v[col] = message[0:1]
+    idx_v[n_col + row] = message[1:2]
+    to_tab = pltpu.make_async_copy(tab_v, tab_s, tab_sem)
+    to_tab.start()
     corr_1[...] = jnp.zeros_like(corr_1)
     corr_2[...] = jnp.zeros_like(corr_2)
     gram_1[...] = jnp.zeros_like(gram_1)
@@ -163,17 +161,19 @@
             back_c[i, CAP] = zero_block
     pl.semaphore_wait(barrier, n_row + n_col - 2)
 
-    idx_r = Exchange("col", lambda p: tab_v.at[p], lambda i: idx_v.at[i], ir_s, ir_r)
-    idx_c = Exchange("row", lambda p: tab_v.at[n_col + p], lambda i: idx_v.at[n_col + i], ic_s, ic_r)
+    idx_r = Exchange("col", lambda p: tab_v.at[0], lambda i: idx_v.at[i], ir_s, ir_r)
+    idx_c = Exchange("row", lambda p: tab_v.at[1], lambda i: idx_v.at[n_col + i], ic_s, ic_r)
     idx_r.start()
     idx_c.start()
-    for b in range(segb):
-        own[0, b] = vec[:, b * TILE:(b + 1) * TILE]
-    idx_c.wait_recv()
-    idx_r.wait_recv()
-    to_smem = pltpu.make_async_copy(idx_v, idx_s, idx_sem)
-    to_smem.start()
-    to_smem.wait()
+    to_tab.wait()
+
+    def place_slots(k, carry):
+        live = k < live_count
+        slot_s[0, k] = jnp.where(live, tab_s[2, 0, rows[0, 0, k]], -1)
+        slot_s[1, k] = jnp.where(live, tab_s[3, 0, cols[0, 0, k]], -1)
+        return carry
+
+    lax.fori_loop(0, slots, place_slots, 0)
 
     def build_pick(line, pick):
         n, wide = pick.shape
@@ -181,7 +181,7 @@
         slot_of, vector_of = lane // nv, lane % nv
 
         def step(k, carry):
-            return jnp.where(slot_of == k, vector_of + nv * tab_s[line, 0, k], carry)
+            return jnp.where(slot_of == k, vector_of + nv * slot_s[line, k], carry)
 
         wanted = lax.fori_loop(0, slots, step, jnp.full((8, wide), -1, jnp.int32))[0:1]
         part = CAP * nv
@@ -195,17 +195,21 @@
 
         lax.fori_loop(0, n // part, fill, 0)
 
-    def split_tiles():
-        for i in range(n_chunks):
-            tile_copies[i].wait()
-
-            def step(k, carry):
-                high, low = split(raw[k])
-                tile_hi[k] = high
-                tile_lo[k] = low
-                return carry
-
-            lax.fori_loop(i * chunk, (i + 1) * chunk, step, 0)
+    build_pick(0, pick_r)
+    build_pick(1, pick_c)
+    for c in vec_copies:
+        c.wait()
+    idx_c.wait_recv()
+    idx_r.wait_recv()
+    to_smem = pltpu.make_async_copy(idx_v, idx_s, idx_sem)
+    to_smem.start()
+    to_smem.wait()
+
+    def needed(i, seg_of, j):
+        return lax.shift_right_logical(idx_s[i, 0, seg_of * segb + j], 3)
+
+    def position(i, seg_of, b):
+        return idx_s[i, 0, seg_of * segb + b] & (NEED - 1)
 
     def split_blocks(n, source, target):
         def step(i, carry):
@@ -217,21 +221,33 @@
 
         lax.fori_loop(0, n, step, 0)
 
-    def multiply(line, blocks, pick, n, out, dot):
-        width = 4 if slots % 4 == 0 else 1
+    def multiply(line, blocks, pick, n, out, dot, fresh):
+        width = 4 if chunk % 4 == 0 else 1
 
         def step(g, carry):
             for u in range(width):
                 k = g * width + u
-                x = blocks[jnp.maximum(tab_s[line, 0, k], 0)]
-                wide = dot(x, tile_hi[k])
-                z = wide[0:nv] + wide[nv:2 * nv] + dot(x[0:nv], tile_lo[k])
+                x = blocks[jnp.maximum(slot_s[line, k], 0)]
+                if fresh:
+                    t_hi, t_lo = split(raw[k])
+                    tile_hi[k] = t_hi
+                    tile_lo[k] = t_lo
+                else:
+                    t_hi, t_lo = tile_hi[k], tile_lo[k]
+                wide = dot(x, t_hi)
+                z = wide[0:nv] + wide[nv:2 * nv] + dot(x[0:nv], t_lo)
                 high, low = split(z)
                 z_hi[k] = high
                 z_lo[k] = low
             return carry
 
-        lax.fori_loop(0, slots // width, step, 0)
+        per = chunk // width
+        if fresh:
+            for i in range(n_chunks):
+                tile_copies[i].wait()
+                lax.fori_loop(i * per, (i + 1) * per, step, 0)
+        else:
+            lax.fori_loop(0, n_chunks * per, step, 0)
         flat = (slots * nv, TILE)
         y = dot_nn(pick[...], z_hi[...].reshape(flat)) + dot_nn(pick[...], z_lo[...].reshape(flat))
         out[...] = y.reshape(n, CAP, nv, TILE)
@@ -252,27 +268,27 @@
 
             def one(p):
                 for j in range(CAP):
-                    send[p, j] = own[which, idx_s[base + p, 0, j]]
+                    send[p, j] = own[which, needed(base + p, me, j)]
                 exchange.make(p, me).start()
 
             each_peer(axis, one)
             for j in range(CAP):
-                got[me, j] = own[which, idx_s[base + me, 0, j]]
+                got[me, j] = own[which, needed(base + me, me, j)]
 
         pack("row", n_col, gather_c, send_c, got_c)
         pack("col", 0, gather_r, send_r, got_r)
         first()
         gather_c.wait_recv()
         split_blocks(n_row, got_c, zc)
-        multiply(n_row + n_col + 1, zc, pick_r, n_col, y_r, dot_nt)
+        multiply(1, zc, pick_r, n_col, y_r, dot_nt, which == 0)
         scatter_r.start()
         for j in range(CAP):
             back_r[col, j] = y_r[col, j]
         after_rows()
         gather_r.wait_recv()
         split_blocks(n_col, got_r, zr)
-        after_gather(got_r, y_r)
-        multiply(n_row + n_col, zr, pick_c, n_row, y_c, dot_nn)
+        after_gather(y_r)
+        multiply(0, zr, pick_c, n_row, y_c, dot_nn, False)
         scatter_c.start()
         for j in range(CAP):
             back_c[row, j] = y_c[row, j]
@@ -282,18 +298,19 @@
         for b in range(segb):
             total = zero_block
             for i in range(n_row):
-                total = total + back_c[i, idx_s[n_col + i, 0, POS + b]]
+                total = total + back_c[i, position(n_col + i, row, b)]
             for i in range(n_col):
-                total = total + back_r[i, idx_s[i, 0, POS + b]]
+                total = total + back_r[i, position(i, col, b)]
             own[which + 1, b] = total
 
-    def setup():
-        build_pick(n_row + n_col, pick_r)
-        build_pick(n_row + n_col + 1, pick_c)
-        split_tiles()
+    def own_correlation():
+        total = jnp.zeros((nv, nv), F32)
+        for b in range(segb):
+            total = total + dot_nt(own[0, b], own[0, b], EXACT)
+        small[0, :, 0:nv] = total
 
     nothing = lambda *unused: None
-    apply(0, setup, nothing, nothing, nothing)
+    apply(0, nothing, own_correlation, nothing, nothing)
 
     corr_row = Exchange("row", lambda p: corr_1.at[row], lambda i: corr_1.at[i], c1_s, c1_r)
     corr_col = Exchange("col", lambda p: corr_2.at[col], lambda i: corr_2.at[i], c2_s, c2_r)
@@ -307,12 +324,16 @@
             total = total + ref[i]
         return total
 
+    def fold(total, n):
+        return total[0:n, 0:n] + total[0:n, n:2 * n] + total[n:2 * n, 0:n] + total[n:2 * n, n:2 * n]
+
     def correlate():
-        total = jnp.zeros((2 * nv, 2 * nv), F32)
+        total = jnp.zeros((4 * nv, 4 * nv), F32)
         for b in range(segb):
-            both = jnp.concatenate([own[0, b], own[1, b]], axis=0)
-            total = total + dot_nt(both, both, EXACT)
-        corr_1[row, :, 0:2 * nv] = total
+            both = jnp.concatenate(split(jnp.concatenate([own[0, b], own[1, b]], axis=0)), axis=0)
+            total = total + dot_nt(both, both)
+        corr_1[row, :, 0:2 * nv] = fold(total, 2 * nv)
+        corr_1[row, 0:nv, 0:nv] = small[0, :, 0:nv]
         corr_row.start()
 
     def correlate_on():
@@ -320,16 +341,22 @@
         corr_2[col] = total_of(corr_1, n_row)
         corr_col.start()
 
-    def gram_terms(got_r, y_r):
+    eye = jnp.where(
+        lax.broadcasted_iota(jnp.int32, (nv, nv), 0) == lax.broadcasted_iota(jnp.int32, (nv, nv), 1),
+        1.0, 0.0,
+    ).astype(F32)
+
+    def gram_terms(y_r):
         def step(i, total):
             for j in range(CAP):
-                total = total + dot_nt(got_r[i, j], y_r[i, j], EXACT)
+                y = jnp.concatenate(split(y_r[i, j]), axis=0)
+                total = total + dot_nt(zr[i * CAP + j], y)
             return total
 
-        gram_1[row, :, 0:nv] = lax.fori_loop(0, n_col, step, jnp.zeros((nv, nv), F32))
+        total = lax.fori_loop(0, n_col, step, jnp.zeros((2 * nv, 2 * nv), F32))
+        half = fold(total, nv)
+        gram_1[row, :, 0:nv] = half + dot_nt(eye, half, EXACT)
         gram_row.start()
-
-    answers = []
 
     def solve():
         gram_row.wait_recv()
@@ -348,24 +375,22 @@
         coeffs_t = dot_nt(second, m, EXACT)
         proj = dot_nt(sums[0:nv], second, EXACT)
         squares = dot_nt(sums[nv:2 * nv], second, EXACT)
-        answers.extend([coeffs_t, proj, squares])
         for b in range(segb):
-            residual[:, b * TILE:(b + 1) * TILE] = own[1, b] - dot_nn(coeffs_t, own[0, b], EXACT)
-
+            out_v[:, b * TILE:(b + 1) * TILE] = own[1, b] - dot_nn(coeffs_t, own[0, b], EXACT)
+        out_copy.start()
+        for b in range(segb):
+            later[b] = dot_nn(coeffs_t, own[1, b], EXACT)
+        rest = dot_nt(dot_nn(coeffs_t, proj, EXACT), coeffs_t, EXACT)
+        rest = rest - dot_nn(coeffs_t, squares, EXACT) - dot_nt(squares, coeffs_t, EXACT)
+        small[1, :, 0:nv] = rest
+
+    out_copy = pltpu.make_async_copy(out_v, residual, out_sem)
     apply(1, correlate, correlate_on, gram_terms, solve)
-    coeffs_t, proj, squares = answers
     for b in range(segb):
-        image[:, b * TILE:(b + 1) * TILE] = own[2, b] - dot_nn(coeffs_t, own[1, b], EXACT)
+        image[:, b * TILE:(b + 1) * TILE] = own[2, b] - later[b]
     gram_col.wait_recv()
-    half = total_of(gram_2, n_col)[:, 0:nv]
-    eye = jnp.where(
-        lax.broadcasted_iota(jnp.int32, (nv, nv), 0) == lax.broadcasted_iota(jnp.int32, (nv, nv), 1),
-        1.0, 0.0,
-    ).astype(F32)
-    whole = half + dot_nt(eye, half, EXACT)
-    whole = whole - dot_nn(coeffs_t, squares, EXACT) - dot_nt(squares, coeffs_t, EXACT)
-    whole = whole + dot_nt(dot_nn(coeffs_t, proj, EXACT), coeffs_t, EXACT)
-    gram[...] = whole / order
+    gram[...] = (total_of(gram_2, n_col)[:, 0:nv] + small[1, :, 0:nv]) / order
+    out_copy.wait()
     for e in exchanges:
         e.wait_send()
 
@@ -374,15 +399,9 @@
     nv, width = vectors.shape
     segb = width // TILE
     slots = tiles.shape[2]
-    lines = n_row + n_col + 2
     smem = pl.BlockSpec(memory_space=pltpu.SMEM)
     vmem = pl.BlockSpec(memory_space=pltpu.VMEM)
-    table = pl.pallas_call(
-        functools.partial(prep_kernel, n_row, n_col, segb),
-        out_shape=jax.ShapeDtypeStruct((lines, 1, 128), jnp.int32),
-        in_specs=[smem] * 3,
-        out_specs=smem,
-    )(tile_rows, tile_cols, counts)
+    anywhere = pl.BlockSpec(memory_space=pl.ANY)
     dma = pltpu.SemaphoreType.DMA
     rb, cb = (n_col, CAP, nv, TILE), (n_row, CAP, nv, TILE)
     most = max(n_row, n_col)
@@ -409,7 +428,16 @@
         pltpu.VMEM((n_col, 2 * nv, 128), F32),
         pltpu.VMEM((n_row, nv, 128), F32),
         pltpu.VMEM((n_col, nv, 128), F32),
+        pltpu.VMEM((4, 1, 128), jnp.int32),
+        pltpu.SMEM((4, 1, 128), jnp.int32),
+        pltpu.SMEM((2, slots), jnp.int32),
+        pltpu.VMEM((nv, width), F32),
+        pltpu.VMEM((segb, nv, TILE), F32),
+        pltpu.VMEM((2, nv, 128), F32),
         dma((slots,)),
+        dma(()),
+        dma(()),
+        dma((segb,)),
         dma(()),
         *one_round,
         *one_round,
@@ -425,13 +453,13 @@
             jax.ShapeDtypeStruct((nv, width), F32),
             jax.ShapeDtypeStruct((nv, nv), F32),
         ),
-        in_specs=[smem, vmem, vmem, pl.BlockSpec(memory_space=pl.ANY)],
-        out_specs=(vmem, vmem, vmem),
+        in_specs=[smem, smem, smem, anywhere, anywhere],
+        out_specs=(anywhere, vmem, vmem),
         scratch_shapes=scratch,
         compiler_params=pltpu.CompilerParams(
             collective_id=0, has_side_effects=True, vmem_limit_bytes=52 * 2**20
         ),
-    )(table, table, vectors, tiles)
+    )(tile_rows, tile_cols, counts, vectors, tiles)
 
 
 def solution(mesh):

time: 66.5 us -> 62.8 us (0.944)
  Pallas kernels: 61.5 us -> 57.2 us
    pallas_call x1 -> x0, Pallas kernels: 4.57 us -> none  [per_device(): pl.pallas_call(functools.partial(prep_kernel, n_row, n_col, segb), out_sh...]
    unnamed x7 -> x9, local copies, waits for them, and re-layouts: 3.46 us -> 4.08 us
where the time goes in v2:
time: 62.8 us; the launch traced here: 62.6 us
  Pallas kernels  57.2 us (91%)
  local copies, waits for them, and re-layouts  4.08 us (6%)
  between operations  1.3 us (2%)
    pallas_call x1, Pallas kernels, per_device(): pl.pallas_call(functools.partial(main_kernel, n_row, n_col, segb, order),...  57.2 us
    unnamed x9, local copies, waits for them, and re-layouts  4.08 us

profile of v2, /device:TPU:0, one launch (start us, length us, event | category | flops | bytes accessed | tf_op | source)
XLA Modules:
  0.0 62.6 jit_solution(13808183601111058524)
XLA Ops:
  1.3 0.0 copy-start
  1.3 0.9 %copy-done = f32[16,1536]{1,0:T(8,128)S(1)} copy-done((f32[16,1536]{1,0:T(8,128)S(1)}, f32[16,1536]{1,0:T(8,128)}, u32[]{:S(2)}) %copy-start) | copy-done | bytes 98328
  2.2 0.0 copy-start.1
  2.2 0.7 %copy-done.1 = s32[1,1,48]{2,1,0:T(1,128)S(1)} copy-done((s32[1,1,48]{2,1,0:T(1,128)S(1)}, s32[1,1,48]{2,1,0:T(1,128)}, u32[]{:S(2)}) %copy-start.1) | copy-done | bytes 216
  2.8 0.0 copy-start.2
  2.8 0.7 %copy-done.2 = s32[1,1,48]{2,1,0:T(1,128)S(1)} copy-done((s32[1,1,48]{2,1,0:T(1,128)S(1)}, s32[1,1,48]{2,1,0:T(1,128)}, u32[]{:S(2)}) %copy-start.2) | copy-done | bytes 216
  3.5 57.2 %shard_map.76 = (f32[16,1536]{1,0:T(8,128)S(1)}, f32[16,1536]{1,0:T(8,128)S(1)}, f32[16,16]{1,0:T(8,128)S(1)}) custom-call(s32[1,1,48]{2,1,0:T(1,128)S(1)} %copy-done.1, s32[1,1,48]{2,1,0:T(1,128)S(1)} %copy-done.2, s32[1,1]{1,0:T(1,128)S(6)} %copy.11.refs_2_, f32[16,1536]{1,0:T(8,128)S(1)} %copy-done, f32[1,1,48,256,256]{4,3,2,1,0:T(8,128)} %refs_4_.1), custom_call_target="tpu_custom_call" | custom-call | tf_op jit(solution)/shard_map/pallas_call | solution.py:449
  60.7 0.6 %copy.12 = f32[16,1536]{1,0:T(8,128)} copy(f32[16,1536]{1,0:T(8,128)S(1)} %get-tuple-element.6) | data formatting | bytes 196608
  61.3 0.6 %copy.13 = f32[16,1536]{1,0:T(8,128)} copy(f32[16,1536]{1,0:T(8,128)S(1)} %get-tuple-element.7) | data formatting | bytes 196608
  62.0 0.6 copy.14
Async XLA Ops:
  1.3 0.9 %copy-start = (f32[16,1536]{1,0:T(8,128)S(1)}, f32[16,1536]{1,0:T(8,128)}, u32[]{:S(2)}) copy-start(f32[16,1536]{1,0:T(8,128)} %refs_3_.1) | copy-start | bytes 294916
  2.2 0.7 %copy-start.1 = (s32[1,1,48]{2,1,0:T(1,128)S(1)}, s32[1,1,48]{2,1,0:T(1,128)}, u32[]{:S(2)}) copy-start(s32[1,1,48]{2,1,0:T(1,128)} %refs_0_.1) | copy-start | bytes 580
  2.8 0.7 %copy-start.2 = (s32[1,1,48]{2,1,0:T(1,128)S(1)}, s32[1,1,48]{2,1,0:T(1,128)}, u32[]{:S(2)}) copy-start(s32[1,1,48]{2,1,0:T(1,128)} %refs_1_.1) | copy-start | bytes 580

commit v3 on v2

--- a/solution.py
+++ b/solution.py
@@ -222,7 +222,7 @@
         lax.fori_loop(0, n, step, 0)
 
     def multiply(line, blocks, pick, n, out, dot, fresh):
-        width = 4 if chunk % 4 == 0 else 1
+        width = chunk
 
         def step(g, carry):
             for u in range(width):
@@ -457,7 +457,7 @@
         out_specs=(anywhere, vmem, vmem),
         scratch_shapes=scratch,
         compiler_params=pltpu.CompilerParams(
-            collective_id=0, has_side_effects=True, vmem_limit_bytes=52 * 2**20
+            collective_id=0, has_side_effects=True, vmem_limit_bytes=60 * 2**20
         ),
     )(tile_rows, tile_cols, counts, vectors, tiles)
 

time: 62.8 us -> 63.8 us (1.016)
  Pallas kernels: 57.2 us -> 57.9 us
    pallas_call x1, Pallas kernels: 57.2 us -> 57.9 us  [per_device(): pl.pallas_call(functools.partial(main_kernel, n_row, n_col, segb, order),...]
    unnamed x9 -> x3, local copies, waits for them, and re-layouts: 4.08 us -> 4.37 us
where the time goes in v3:
time: 63.8 us; the launch traced here: 63.6 us
  Pallas kernels  57.9 us (91%)
  local copies, waits for them, and re-layouts  4.37 us (7%)
  between operations  1.29 us (2%)
    pallas_call x1, Pallas kernels, per_device(): pl.pallas_call(functools.partial(main_kernel, n_row, n_col, segb, order),...  57.9 us
    unnamed x3, local copies, waits for them, and re-layouts  4.37 us

profile of v3, /device:TPU:0, one launch (start us, length us, event | category | flops | bytes accessed | tf_op | source)
XLA Modules:
  0.0 63.6 jit_solution(17705026805115708661)
XLA Ops:
  1.3 57.9 %shard_map.76 = (f32[16,1536]{1,0:T(8,128)}, f32[16,1536]{1,0:T(8,128)}, f32[16,16]{1,0:T(8,128)}) custom-call(s32[1,1,48]{2,1,0:T(1,128)} %refs_0_.1, s32[1,1,48]{2,1,0:T(1,128)} %refs_1_.1, s32[1,1]{1,0:T(1,128)S(6)} %copy.11.refs_2_, f32[16,1536]{1,0:T(8,128)} %refs_3_.1, f32[1,1,48,256,256]{4,3,2,1,0:T(8,128)} %refs_4_.1), custom_call_target="tpu_custom_call" | custom-call | tf_op jit(solution)/shard_map/pallas_call | solution.py:449
  59.2 1.5 %copy.12 = f32[16,1536]{1,0:T(8,128)} copy(f32[16,1536]{1,0:T(8,128)} %get-tuple-element.6) | data formatting | bytes 196608
  60.8 1.5 %copy.13 = f32[16,1536]{1,0:T(8,128)} copy(f32[16,1536]{1,0:T(8,128)} %get-tuple-element.7) | data formatting | bytes 196608
  62.3 1.3 %copy.14 = f32[16,16]{1,0:T(8,128)} copy(f32[16,16]{1,0:T(8,128)} %get-tuple-element.8) | data formatting | bytes 2048

commit v4 on v3

--- a/solution.py
+++ b/solution.py
@@ -33,16 +33,43 @@
     return high, (x - high.astype(F32)).astype(BF16)
 
 
+def iota(shape, dim):
+    return lax.broadcasted_iota(jnp.int32, shape, dim)
+
+
+def one_hot(condition):
+    return jnp.where(condition, 1.0, 0.0).astype(F32)
+
+
+def spread(n):
+    per = 128 // n
+    lanes = one_hot(iota((n, 128), 1) % n == iota((n, 128), 0))
+    kept = one_hot(iota((n, 128), 1) // n == iota((n, 128), 0) % per)
+    lines = one_hot(iota((n // per, n), 1) // per == iota((n // per, n), 0))
+    back = one_hot(iota((n, n // per), 0) // per == iota((n, n // per), 1))
+    return lanes, kept, lines, back
+
+
+def pack_square(x):
+    lanes, kept, lines, _ = spread(x.shape[0])
+    return dot_nn(lines, dot_nn(x, lanes, EXACT) * kept, EXACT)
+
+
+def unpack_square(x, n):
+    lanes, kept, _, back = spread(n)
+    return dot_nt(dot_nn(back, x, EXACT) * kept, lanes, EXACT)
+
+
 def main_kernel(n_row, n_col, segb, order, *refs):
-    (rows, cols, count, vec, tiles, residual, image, gram) = refs[:8]
+    (rows_hbm, cols_hbm, count, vec, tiles, residual, image, gram) = refs[:8]
     refs = refs[8:]
     (
         raw, tile_hi, tile_lo, pick_r, pick_c, z_hi, z_lo, idx_v, idx_s, own,
         zr, zc, corr_1, corr_2, gram_1, gram_2, tab_v, tab_s, slot_s, out_v, later, small,
-        tile_sem, idx_sem, tab_sem, vec_sem, out_sem,
-    ) = refs[:27]
-    rounds = [refs[27:40], refs[40:53]]
-    (ir_s, ir_r, ic_s, ic_r, c1_s, c1_r, c2_s, c2_r, g1_s, g1_r, g2_s, g2_r) = refs[53:65]
+        tile_sem, idx_sem, tab_sem, vec_sem, out_sem, rows, cols, list_sem,
+    ) = refs[:30]
+    rounds = [refs[30:43], refs[43:56]]
+    (ir_s, ir_r, ic_s, ic_r, c1_s, c1_r, c2_s, c2_r, g1_s, g1_r, g2_s, g2_r) = refs[56:68]
     nv = vec.shape[0]
     slots = raw.shape[0]
     row = lax.axis_index("row")
@@ -98,7 +125,11 @@
         pltpu.make_async_copy(vec.at[:, pl.ds(b * TILE, TILE)], own.at[0, b], vec_sem.at[b])
         for b in range(segb)
     ]
-    for c in vec_copies + tile_copies:
+    list_copies = [
+        pltpu.make_async_copy(rows_hbm, rows, list_sem.at[0]),
+        pltpu.make_async_copy(cols_hbm, cols, list_sem.at[1]),
+    ]
+    for c in list_copies + vec_copies + tile_copies:
         c.start()
 
     barrier = pltpu.get_barrier_semaphore()
@@ -130,6 +161,8 @@
         return named
 
     unroll = 8 if slots % 8 == 0 else 1
+    for c in list_copies:
+        c.wait()
     named = lax.fori_loop(0, slots // unroll, touch, jnp.zeros((8, 128), jnp.int32))
     rank = jnp.zeros((8, 128), jnp.int32)
     for d in range(1, segb):
@@ -148,10 +181,6 @@
     idx_v[n_col + row] = message[1:2]
     to_tab = pltpu.make_async_copy(tab_v, tab_s, tab_sem)
     to_tab.start()
-    corr_1[...] = jnp.zeros_like(corr_1)
-    corr_2[...] = jnp.zeros_like(corr_2)
-    gram_1[...] = jnp.zeros_like(gram_1)
-    gram_2[...] = jnp.zeros_like(gram_2)
     zero_block = jnp.zeros((nv, TILE), F32)
     for r in rounds:
         back_r, back_c = r[4], r[5]
@@ -254,7 +283,7 @@
 
     exchanges = [idx_r, idx_c]
 
-    def apply(which, first, after_rows, after_gather, after_columns):
+    def apply(which, first, before_rows, after_rows, after_gather, after_columns):
         send_r, send_c, got_r, got_c, back_r, back_c, y_r, y_c = rounds[which][:8]
         gr_s, gc_s, br_s, bc_s, rr = rounds[which][8:]
         gather_r = Exchange("col", lambda p: send_r.at[p], lambda i: got_r.at[i], gr_s, rr.at[0])
@@ -279,6 +308,7 @@
         pack("col", 0, gather_r, send_r, got_r)
         first()
         gather_c.wait_recv()
+        before_rows()
         split_blocks(n_row, got_c, zc)
         multiply(1, zc, pick_r, n_col, y_r, dot_nt, which == 0)
         scatter_r.start()
@@ -307,10 +337,11 @@
         total = jnp.zeros((nv, nv), F32)
         for b in range(segb):
             total = total + dot_nt(own[0, b], own[0, b], EXACT)
-        small[0, :, 0:nv] = total
+        small[0] = jnp.zeros_like(small[0])
+        small[0, 0:nv, 0:nv] = total
 
     nothing = lambda *unused: None
-    apply(0, nothing, own_correlation, nothing, nothing)
+    apply(0, nothing, nothing, own_correlation, nothing, nothing)
 
     corr_row = Exchange("row", lambda p: corr_1.at[row], lambda i: corr_1.at[i], c1_s, c1_r)
     corr_col = Exchange("col", lambda p: corr_2.at[col], lambda i: corr_2.at[i], c2_s, c2_r)
@@ -332,8 +363,9 @@
         for b in range(segb):
             both = jnp.concatenate(split(jnp.concatenate([own[0, b], own[1, b]], axis=0)), axis=0)
             total = total + dot_nt(both, both)
-        corr_1[row, :, 0:2 * nv] = fold(total, 2 * nv)
-        corr_1[row, 0:nv, 0:nv] = small[0, :, 0:nv]
+        total = fold(total, 2 * nv)
+        head = (iota((2 * nv, 2 * nv), 0) < nv) & (iota((2 * nv, 2 * nv), 1) < nv)
+        corr_1[row] = pack_square(jnp.where(head, small[0, :, 0:2 * nv], total))
         corr_row.start()
 
     def correlate_on():
@@ -355,7 +387,7 @@
 
         total = lax.fori_loop(0, n_col, step, jnp.zeros((2 * nv, 2 * nv), F32))
         half = fold(total, nv)
-        gram_1[row, :, 0:nv] = half + dot_nt(eye, half, EXACT)
+        gram_1[row] = pack_square(half + dot_nt(eye, half, EXACT))
         gram_row.start()
 
     def solve():
@@ -363,8 +395,8 @@
         gram_2[col] = total_of(gram_1, n_row)
         gram_col.start()
         corr_col.wait_recv()
-        sums = total_of(corr_2, n_col)
-        lanes = sums.shape[1]
+        sums = unpack_square(total_of(corr_2, n_col), 2 * nv)
+        lanes = 2 * nv
         m = sums[0:nv]
         line = lax.broadcasted_iota(jnp.int32, (nv, lanes), 0)
         lane = lax.broadcasted_iota(jnp.int32, (nv, lanes), 1)
@@ -382,14 +414,14 @@
             later[b] = dot_nn(coeffs_t, own[1, b], EXACT)
         rest = dot_nt(dot_nn(coeffs_t, proj, EXACT), coeffs_t, EXACT)
         rest = rest - dot_nn(coeffs_t, squares, EXACT) - dot_nt(squares, coeffs_t, EXACT)
-        small[1, :, 0:nv] = rest
+        small[1, 0:nv, 0:nv] = rest
 
     out_copy = pltpu.make_async_copy(out_v, residual, out_sem)
-    apply(1, correlate, correlate_on, gram_terms, solve)
+    apply(1, correlate, correlate_on, nothing, gram_terms, solve)
     for b in range(segb):
         image[:, b * TILE:(b + 1) * TILE] = own[2, b] - later[b]
     gram_col.wait_recv()
-    gram[...] = (total_of(gram_2, n_col)[:, 0:nv] + small[1, :, 0:nv]) / order
+    gram[...] = (unpack_square(total_of(gram_2, n_col), nv) + small[1, 0:nv, 0:nv]) / order
     out_copy.wait()
     for e in exchanges:
         e.wait_send()
@@ -402,6 +434,8 @@
     smem = pl.BlockSpec(memory_space=pltpu.SMEM)
     vmem = pl.BlockSpec(memory_space=pltpu.VMEM)
     anywhere = pl.BlockSpec(memory_space=pl.ANY)
+    hbm = pl.BlockSpec(memory_space=pltpu.HBM)
+    in_hbm = lambda x: pltpu.with_memory_space_constraint(x, pltpu.HBM)
     dma = pltpu.SemaphoreType.DMA
     rb, cb = (n_col, CAP, nv, TILE), (n_row, CAP, nv, TILE)
     most = max(n_row, n_col)
@@ -424,21 +458,24 @@
         pltpu.VMEM((3, segb, nv, TILE), F32),
         pltpu.VMEM((n_col * CAP, 2 * nv, TILE), BF16),
         pltpu.VMEM((n_row * CAP, 2 * nv, TILE), BF16),
-        pltpu.VMEM((n_row, 2 * nv, 128), F32),
-        pltpu.VMEM((n_col, 2 * nv, 128), F32),
-        pltpu.VMEM((n_row, nv, 128), F32),
-        pltpu.VMEM((n_col, nv, 128), F32),
+        pltpu.VMEM((n_row, 4 * nv * nv // 128, 128), F32),
+        pltpu.VMEM((n_col, 4 * nv * nv // 128, 128), F32),
+        pltpu.VMEM((n_row, nv * nv // 128, 128), F32),
+        pltpu.VMEM((n_col, nv * nv // 128, 128), F32),
         pltpu.VMEM((4, 1, 128), jnp.int32),
         pltpu.SMEM((4, 1, 128), jnp.int32),
         pltpu.SMEM((2, slots), jnp.int32),
         pltpu.VMEM((nv, width), F32),
         pltpu.VMEM((segb, nv, TILE), F32),
-        pltpu.VMEM((2, nv, 128), F32),
+        pltpu.VMEM((2, 2 * nv, 128), F32),
         dma((slots,)),
         dma(()),
         dma(()),
         dma((segb,)),
         dma(()),
+        pltpu.SMEM((1, 1, slots), jnp.int32),
+        pltpu.SMEM((1, 1, slots), jnp.int32),
+        dma((2,)),
         *one_round,
         *one_round,
         dma((n_col,)), dma((n_col,)), dma((n_row,)), dma((n_row,)),
@@ -453,13 +490,13 @@
             jax.ShapeDtypeStruct((nv, width), F32),
             jax.ShapeDtypeStruct((nv, nv), F32),
         ),
-        in_specs=[smem, smem, smem, anywhere, anywhere],
+        in_specs=[hbm, hbm, smem, hbm, hbm],
         out_specs=(anywhere, vmem, vmem),
         scratch_shapes=scratch,
         compiler_params=pltpu.CompilerParams(
-            collective_id=0, has_side_effects=True, vmem_limit_bytes=60 * 2**20
+            collective_id=0, has_side_effects=True, vmem_limit_bytes=52 * 2**20
         ),
-    )(tile_rows, tile_cols, counts, vectors, tiles)
+    )(in_hbm(tile_rows), in_hbm(tile_cols), counts, in_hbm(vectors), tiles)
 
 
 def solution(mesh):

time: 63.8 us -> 60.6 us (0.950)
  local copies, waits for them, and re-layouts: 4.37 us -> 1.88 us
    unnamed x3, local copies, waits for them, and re-layouts: 4.37 us -> 1.88 us
where the time goes in v4:
time: 60.6 us; the launch traced here: 60.5 us
  Pallas kernels  57.3 us (95%)
  local copies, waits for them, and re-layouts  1.88 us (3%)
  between operations  1.29 us (2%)
    pallas_call x1, Pallas kernels, per_device(): pl.pallas_call(functools.partial(main_kernel, n_row, n_col, segb, order),...  57.3 us
    unnamed x3, local copies, waits for them, and re-layouts  1.88 us

profile of v4, /device:TPU:0, one launch (start us, length us, event | category | flops | bytes accessed | tf_op | source)
XLA Modules:
  0.0 60.5 jit_solution(3019484794649174024)
XLA Ops:
  1.3 57.3 %shard_map.76 = (f32[16,1536]{1,0:T(8,128)S(1)}, f32[16,1536]{1,0:T(8,128)S(1)}, f32[16,16]{1,0:T(8,128)S(1)}) custom-call(s32[1,1,48]{2,1,0:T(1,128)} %refs_0_.1, s32[1,1,48]{2,1,0:T(1,128)} %refs_1_.1, s32[1,1]{1,0:T(1,128)S(6)} %copy.11.refs_2_, f32[16,1536]{1,0:T(8,128)} %refs_3_.1, f32[1,1,48,256,256]{4,3,2,1,0:T(8,128)} %refs_4_.1), custom_call_target="tpu_custom_call" | custom-call | tf_op jit(solution)/shard_map/pallas_call | solution.py:486
  58.6 0.6 %copy.12 = f32[16,1536]{1,0:T(8,128)} copy(f32[16,1536]{1,0:T(8,128)S(1)} %get-tuple-element.6) | data formatting | bytes 196608
  59.3 0.6 %copy.13 = f32[16,1536]{1,0:T(8,128)} copy(f32[16,1536]{1,0:T(8,128)S(1)} %get-tuple-element.7) | data formatting | bytes 196608
  59.9 0.6 copy.14

commit v5 on v4

--- a/solution.py
+++ b/solution.py
@@ -68,8 +68,8 @@
         zr, zc, corr_1, corr_2, gram_1, gram_2, tab_v, tab_s, slot_s, out_v, later, small,
         tile_sem, idx_sem, tab_sem, vec_sem, out_sem, rows, cols, list_sem,
     ) = refs[:30]
-    rounds = [refs[30:43], refs[43:56]]
-    (ir_s, ir_r, ic_s, ic_r, c1_s, c1_r, c2_s, c2_r, g1_s, g1_r, g2_s, g2_r) = refs[56:68]
+    rounds = [refs[30:45], refs[45:60]]
+    (ir_s, ir_r, ic_s, ic_r, c1_s, c1_r, c2_s, c2_r, g1_s, g1_r, g2_s, g2_r) = refs[60:72]
     nv = vec.shape[0]
     slots = raw.shape[0]
     row = lax.axis_index("row")
@@ -83,7 +83,14 @@
         n, me, device = axes[axis]
 
         def step(d, carry):
-            body(lax.rem(me + d, n))
+            if n & (n - 1):
+                body(lax.rem(me + d, n))
+            else:
+                peer, bit = me, 1
+                while bit < n:
+                    peer = peer + ((n - d) // bit % 2) * (1 - 2 * (me // bit % 2)) * bit
+                    bit *= 2
+                body(peer)
             return carry
 
         lax.fori_loop(1, n, step, 0)
@@ -181,13 +188,14 @@
     idx_v[n_col + row] = message[1:2]
     to_tab = pltpu.make_async_copy(tab_v, tab_s, tab_sem)
     to_tab.start()
-    zero_block = jnp.zeros((nv, TILE), F32)
+    part_nv = nv // 2
+    zero_block = jnp.zeros((part_nv, TILE), F32)
     for r in rounds:
-        back_r, back_c = r[4], r[5]
-        for i in range(n_col):
-            back_r[i, CAP] = zero_block
-        for i in range(n_row):
-            back_c[i, CAP] = zero_block
+        for h in range(2):
+            for i in range(n_col):
+                r[4 + h][i, CAP] = zero_block
+            for i in range(n_row):
+                r[6 + h][i, CAP] = zero_block
     pl.semaphore_wait(barrier, n_row + n_col - 2)
 
     idx_r = Exchange("col", lambda p: tab_v.at[0], lambda i: idx_v.at[i], ir_s, ir_r)
@@ -283,55 +291,79 @@
 
     exchanges = [idx_r, idx_c]
 
-    def apply(which, first, before_rows, after_rows, after_gather, after_columns):
-        send_r, send_c, got_r, got_c, back_r, back_c, y_r, y_c = rounds[which][:8]
-        gr_s, gc_s, br_s, bc_s, rr = rounds[which][8:]
-        gather_r = Exchange("col", lambda p: send_r.at[p], lambda i: got_r.at[i], gr_s, rr.at[0])
-        gather_c = Exchange("row", lambda p: send_c.at[p], lambda i: got_c.at[i], gc_s, rr.at[1])
-        scatter_r = Exchange("col", lambda p: y_r.at[p], lambda i: back_r.at[i, pl.ds(0, CAP)], br_s, rr.at[2])
-        scatter_c = Exchange("row", lambda p: y_c.at[p], lambda i: back_c.at[i, pl.ds(0, CAP)], bc_s, rr.at[3])
-        exchanges.extend([gather_r, gather_c, scatter_r, scatter_c])
-
-        def pack(axis, base, exchange, send, got):
-            n, me, device = axes[axis]
-
-            def one(p):
+    class Round:
+        def __init__(self, which):
+            self.which = which
+            send_r, send_c, got_r, got_c, ra, rb, ca, cb, y_r, y_c = rounds[which][:10]
+            gr_s, gc_s, br_s, bc_s, arrived = rounds[which][10:]
+            self.send_r, self.send_c, self.got_r, self.got_c = send_r, send_c, got_r, got_c
+            self.back_r, self.back_c, self.y_r, self.y_c = (ra, rb), (ca, cb), y_r, y_c
+
+            def half(axis, source, target, send, h, at):
+                e = Exchange(axis, source, target, send.at[h], arrived.at[2 * at + h])
+                exchanges.append(e)
+                return e
+
+            def of(h):
+                return pl.ds(h * part_nv, part_nv)
+
+            both = range(2)
+            self.gather_r = [half("col", lambda p, h=h: send_r.at[p, :, of(h)], lambda i, h=h: got_r.at[i, :, of(h)], gr_s, h, 0) for h in both]
+            self.gather_c = [half("row", lambda p, h=h: send_c.at[p, :, of(h)], lambda i, h=h: got_c.at[i, :, of(h)], gc_s, h, 1) for h in both]
+            self.scatter_r = [half("col", lambda p, h=h: y_r.at[p, :, of(h)], lambda i, h=h: self.back_r[h].at[i, pl.ds(0, CAP)], br_s, h, 2) for h in both]
+            self.scatter_c = [half("row", lambda p, h=h: y_c.at[p, :, of(h)], lambda i, h=h: self.back_c[h].at[i, pl.ds(0, CAP)], bc_s, h, 3) for h in both]
+
+        def pack(self, h):
+            rows_of = slice(h * part_nv, (h + 1) * part_nv)
+            for axis, base, exchange, send, got in (
+                ("row", n_col, self.gather_c[h], self.send_c, self.got_c),
+                ("col", 0, self.gather_r[h], self.send_r, self.got_r),
+            ):
+                me = axes[axis][1]
+
+                def one(p):
+                    for j in range(CAP):
+                        send[p, j, rows_of] = own[self.which, needed(base + p, me, j), rows_of]
+                    exchange.make(p, me).start()
+
+                each_peer(axis, one)
                 for j in range(CAP):
-                    send[p, j] = own[which, needed(base + p, me, j)]
-                exchange.make(p, me).start()
-
-            each_peer(axis, one)
-            for j in range(CAP):
-                got[me, j] = own[which, needed(base + me, me, j)]
-
-        pack("row", n_col, gather_c, send_c, got_c)
-        pack("col", 0, gather_r, send_r, got_r)
-        first()
-        gather_c.wait_recv()
-        before_rows()
-        split_blocks(n_row, got_c, zc)
-        multiply(1, zc, pick_r, n_col, y_r, dot_nt, which == 0)
-        scatter_r.start()
-        for j in range(CAP):
-            back_r[col, j] = y_r[col, j]
-        after_rows()
-        gather_r.wait_recv()
-        split_blocks(n_col, got_r, zr)
-        after_gather(y_r)
-        multiply(0, zr, pick_c, n_row, y_c, dot_nn, False)
-        scatter_c.start()
-        for j in range(CAP):
-            back_c[row, j] = y_c[row, j]
-        after_columns()
-        scatter_c.wait_recv()
-        scatter_r.wait_recv()
-        for b in range(segb):
-            total = zero_block
-            for i in range(n_row):
-                total = total + back_c[i, position(n_col + i, row, b)]
-            for i in range(n_col):
-                total = total + back_r[i, position(i, col, b)]
-            own[which + 1, b] = total
+                    got[me, j, rows_of] = own[self.which, needed(base + me, me, j), rows_of]
+
+        def scatter(self, exchange, back, y, me):
+            for h in range(2):
+                exchange[h].start()
+            for h in range(2):
+                for j in range(CAP):
+                    back[h][me, j] = y[me, j, h * part_nv:(h + 1) * part_nv]
+
+        def apply(self, first, before_rows, after_rows, after_gather, after_columns, after_half):
+            first()
+            for h in range(2):
+                self.gather_c[h].wait_recv()
+            before_rows()
+            split_blocks(n_row, self.got_c, zc)
+            multiply(1, zc, pick_r, n_col, self.y_r, dot_nt, self.which == 0)
+            self.scatter(self.scatter_r, self.back_r, self.y_r, col)
+            after_rows()
+            for h in range(2):
+                self.gather_r[h].wait_recv()
+            split_blocks(n_col, self.got_r, zr)
+            after_gather(self.y_r)
+            multiply(0, zr, pick_c, n_row, self.y_c, dot_nn, False)
+            self.scatter(self.scatter_c, self.back_c, self.y_c, row)
+            after_columns()
+            for h in range(2):
+                self.scatter_c[h].wait_recv()
+                self.scatter_r[h].wait_recv()
+                for b in range(segb):
+                    total = zero_block
+                    for i in range(n_row):
+                        total = total + self.back_c[h][i, position(n_col + i, row, b)]
+                    for i in range(n_col):
+                        total = total + self.back_r[h][i, position(i, col, b)]
+                    own[self.which + 1, b, h * part_nv:(h + 1) * part_nv] = total
+                after_half(h)
 
     def own_correlation():
         total = jnp.zeros((nv, nv), F32)
@@ -341,7 +373,10 @@
         small[0, 0:nv, 0:nv] = total
 
     nothing = lambda *unused: None
-    apply(0, nothing, nothing, own_correlation, nothing, nothing)
+    one, two = Round(0), Round(1)
+    for h in range(2):
+        one.pack(h)
+    one.apply(nothing, nothing, own_correlation, nothing, nothing, two.pack)
 
     corr_row = Exchange("row", lambda p: corr_1.at[row], lambda i: corr_1.at[i], c1_s, c1_r)
     corr_col = Exchange("col", lambda p: corr_2.at[col], lambda i: corr_2.at[i], c2_s, c2_r)
@@ -417,7 +452,7 @@
         small[1, 0:nv, 0:nv] = rest
 
     out_copy = pltpu.make_async_copy(out_v, residual, out_sem)
-    apply(1, correlate, correlate_on, nothing, gram_terms, solve)
+    two.apply(correlate, correlate_on, nothing, gram_terms, solve, nothing)
     for b in range(segb):
         image[:, b * TILE:(b + 1) * TILE] = own[2, b] - later[b]
     gram_col.wait_recv()
@@ -441,9 +476,10 @@
     most = max(n_row, n_col)
     one_round = [
         pltpu.VMEM(rb, F32), pltpu.VMEM(cb, F32), pltpu.VMEM(rb, F32), pltpu.VMEM(cb, F32),
-        pltpu.VMEM((n_col, CAP + 1, nv, TILE), F32), pltpu.VMEM((n_row, CAP + 1, nv, TILE), F32),
+        *[pltpu.VMEM((n_col, CAP + 1, nv // 2, TILE), F32)] * 2,
+        *[pltpu.VMEM((n_row, CAP + 1, nv // 2, TILE), F32)] * 2,
         pltpu.VMEM(rb, F32), pltpu.VMEM(cb, F32),
-        dma((n_col,)), dma((n_row,)), dma((n_col,)), dma((n_row,)), dma((4, most)),
+        dma((2, n_col)), dma((2, n_row)), dma((2, n_col)), dma((2, n_row)), dma((8, most)),
     ]
     scratch = [
         pltpu.VMEM((slots, TILE, TILE), F32),

time: 60.6 us -> 58.8 us (0.970)
  Pallas kernels: 57.3 us -> 55.5 us
    pallas_call x1, Pallas kernels: 57.3 us -> 55.5 us  [per_device(): pl.pallas_call(functools.partial(main_kernel, n_row, n_col, segb, order),...]
where the time goes in v5:
time: 58.8 us; the launch traced here: 58.7 us
  Pallas kernels  55.5 us (94%)
  local copies, waits for them, and re-layouts  1.88 us (3%)
  between operations  1.29 us (2%)
    pallas_call x1, Pallas kernels, per_device(): pl.pallas_call(functools.partial(main_kernel, n_row, n_col, segb, order),...  55.5 us
    unnamed x3, local copies, waits for them, and re-layouts  1.88 us

profile of v5, /device:TPU:0, one launch (start us, length us, event | category | flops | bytes accessed | tf_op | source)
XLA Modules:
  0.0 58.7 jit_solution(8999953022288652298)
XLA Ops:
  1.3 55.5 %shard_map.76 = (f32[16,1536]{1,0:T(8,128)S(1)}, f32[16,1536]{1,0:T(8,128)S(1)}, f32[16,16]{1,0:T(8,128)S(1)}) custom-call(s32[1,1,48]{2,1,0:T(1,128)} %refs_0_.1, s32[1,1,48]{2,1,0:T(1,128)} %refs_1_.1, s32[1,1]{1,0:T(1,128)S(6)} %copy.11.refs_2_, f32[16,1536]{1,0:T(8,128)} %refs_3_.1, f32[1,1,48,256,256]{4,3,2,1,0:T(8,128)} %refs_4_.1), custom_call_target="tpu_custom_call" | custom-call | tf_op jit(solution)/shard_map/pallas_call | solution.py:522
  56.8 0.6 %copy.12 = f32[16,1536]{1,0:T(8,128)} copy(f32[16,1536]{1,0:T(8,128)S(1)} %get-tuple-element.6) | data formatting | bytes 196608
  57.4 0.6 %copy.13 = f32[16,1536]{1,0:T(8,128)} copy(f32[16,1536]{1,0:T(8,128)S(1)} %get-tuple-element.7) | data formatting | bytes 196608
  58.1 0.6 %copy.14 = f32[16,16]{1,0:T(8,128)} copy(f32[16,16]{1,0:T(8,128)S(1)} %get-tuple-element.8) | data formatting | bytes 2048

commit v6 on v5

--- a/solution.py
+++ b/solution.py
@@ -258,33 +258,35 @@
 
         lax.fori_loop(0, n, step, 0)
 
-    def multiply(line, blocks, pick, n, out, dot, fresh):
-        width = chunk
+    def split_tiles():
+        def step(g, carry):
+            for u in range(pair):
+                high, low = split(raw[g * pair + u])
+                tile_hi[g * pair + u] = high
+                tile_lo[g * pair + u] = low
+            return carry
+
+        pair = 2 if chunk % 2 == 0 else 1
+        per = chunk // pair
+        for i in range(n_chunks):
+            tile_copies[i].wait()
+            lax.fori_loop(i * per, (i + 1) * per, step, 0)
+
+    def multiply(line, blocks, pick, n, out, dot):
+        width = 16 if slots % 16 == 0 else 1
 
         def step(g, carry):
             for u in range(width):
                 k = g * width + u
                 x = blocks[jnp.maximum(slot_s[line, k], 0)]
-                if fresh:
-                    t_hi, t_lo = split(raw[k])
-                    tile_hi[k] = t_hi
-                    tile_lo[k] = t_lo
-                else:
-                    t_hi, t_lo = tile_hi[k], tile_lo[k]
-                wide = dot(x, t_hi)
-                z = wide[0:nv] + wide[nv:2 * nv] + dot(x[0:nv], t_lo)
+                wide = dot(x, tile_hi[k])
+                z = wide[0:nv] + wide[nv:2 * nv] + dot(x[0:nv], tile_lo[k])
                 high, low = split(z)
                 z_hi[k] = high
                 z_lo[k] = low
             return carry
 
-        per = chunk // width
-        if fresh:
-            for i in range(n_chunks):
-                tile_copies[i].wait()
-                lax.fori_loop(i * per, (i + 1) * per, step, 0)
-        else:
-            lax.fori_loop(0, n_chunks * per, step, 0)
+        lax.fori_loop(0, slots // width, step, 0)
         flat = (slots * nv, TILE)
         y = dot_nn(pick[...], z_hi[...].reshape(flat)) + dot_nn(pick[...], z_lo[...].reshape(flat))
         out[...] = y.reshape(n, CAP, nv, TILE)
@@ -337,20 +339,20 @@
                 for j in range(CAP):
                     back[h][me, j] = y[me, j, h * part_nv:(h + 1) * part_nv]
 
-        def apply(self, first, before_rows, after_rows, after_gather, after_columns, after_half):
+        def apply(self, first, before_scatter, after_rows, after_gather, after_columns, after_half):
             first()
             for h in range(2):
                 self.gather_c[h].wait_recv()
-            before_rows()
             split_blocks(n_row, self.got_c, zc)
-            multiply(1, zc, pick_r, n_col, self.y_r, dot_nt, self.which == 0)
+            multiply(1, zc, pick_r, n_col, self.y_r, dot_nt)
+            before_scatter()
             self.scatter(self.scatter_r, self.back_r, self.y_r, col)
             after_rows()
             for h in range(2):
                 self.gather_r[h].wait_recv()
             split_blocks(n_col, self.got_r, zr)
             after_gather(self.y_r)
-            multiply(0, zr, pick_c, n_row, self.y_c, dot_nn, False)
+            multiply(0, zr, pick_c, n_row, self.y_c, dot_nn)
             self.scatter(self.scatter_c, self.back_c, self.y_c, row)
             after_columns()
             for h in range(2):
@@ -376,7 +378,7 @@
     one, two = Round(0), Round(1)
     for h in range(2):
         one.pack(h)
-    one.apply(nothing, nothing, own_correlation, nothing, nothing, two.pack)
+    one.apply(split_tiles, nothing, own_correlation, nothing, nothing, two.pack)
 
     corr_row = Exchange("row", lambda p: corr_1.at[row], lambda i: corr_1.at[i], c1_s, c1_r)
     corr_col = Exchange("col", lambda p: corr_2.at[col], lambda i: corr_2.at[i], c2_s, c2_r)
@@ -460,6 +462,14 @@
     out_copy.wait()
     for e in exchanges:
         e.wait_send()
+
+
+def hand_on(*refs):
+    copies = [pltpu.make_async_copy(refs[i], refs[3 + i], refs[6].at[i]) for i in range(3)]
+    for c in copies:
+        c.start()
+    for c in copies:
+        c.wait()
 
 
 def per_device(n_row, n_col, vectors, tiles, tile_rows, tile_cols, counts):
@@ -519,7 +529,7 @@
         dma((n_row,)), dma((n_row,)), dma((n_col,)), dma((n_col,)),
     ]
     order = width * n_row * n_col
-    return pl.pallas_call(
+    results = pl.pallas_call(
         functools.partial(main_kernel, n_row, n_col, segb, order),
         out_shape=(
             jax.ShapeDtypeStruct((nv, width), F32),
@@ -533,6 +543,13 @@
             collective_id=0, has_side_effects=True, vmem_limit_bytes=52 * 2**20
         ),
     )(in_hbm(tile_rows), in_hbm(tile_cols), counts, in_hbm(vectors), tiles)
+    return pl.pallas_call(
+        hand_on,
+        out_shape=tuple(jax.ShapeDtypeStruct(x.shape, x.dtype) for x in results),
+        in_specs=[anywhere] * 3,
+        out_specs=(hbm,) * 3,
+        scratch_shapes=[dma((3,))],
+    )(*results)
 
 
 def solution(mesh):

time: 58.8 us -> 64.6 us (1.099)
  Pallas kernels: 55.5 us -> 61.3 us
    pallas_call x0 -> x1, Pallas kernels: none -> 7.33 us  [per_device(): pl.pallas_call(hand_on, out_shape=tuple((jax.ShapeDtypeStruct(x.shape, x....]
    pallas_call x1, Pallas kernels: 55.5 us -> 54 us  [per_device(): pl.pallas_call(functools.partial(main_kernel, n_row, n_col, segb, order),...]
    unnamed x3 -> x6, local copies, waits for them, and re-layouts: 1.88 us -> 1.84 us
where the time goes in v6:
time: 64.6 us; the launch traced here: 64.4 us
  Pallas kernels  61.3 us (95%)
  local copies, waits for them, and re-layouts  1.84 us (3%)
  between operations  1.3 us (2%)
    pallas_call x1, Pallas kernels, per_device(): pl.pallas_call(functools.partial(main_kernel, n_row, n_col, segb, order),...  54 us
    pallas_call x1, Pallas kernels, per_device(): pl.pallas_call(hand_on, out_shape=tuple((jax.ShapeDtypeStruct(x.shape, x....  7.33 us
    unnamed x6, local copies, waits for them, and re-layouts  1.84 us

profile of v6, /device:TPU:0, one launch (start us, length us, event | category | flops | bytes accessed | tf_op | source)
XLA Modules:
  0.0 64.4 jit_solution(12021841413155657081)
XLA Ops:
  1.3 54.0 %shard_map.76 = (f32[16,1536]{1,0:T(8,128)S(1)}, f32[16,1536]{1,0:T(8,128)S(1)}, f32[16,16]{1,0:T(8,128)S(1)}) custom-call(s32[1,1,48]{2,1,0:T(1,128)} %refs_0_.1, s32[1,1,48]{2,1,0:T(1,128)} %refs_1_.1, s32[1,1]{1,0:T(1,128)S(6)} %copy.8.refs_2_, f32[16,1536]{1,0:T(8,128)} %refs_3_.1, f32[1,1,48,256,256]{4,3,2,1,0:T(8,128)} %refs_4_.1), custom_call_target="tpu_custom_call" | custom-call | tf_op jit(solution)/shard_map/pallas_call | solution.py:532
  55.2 0.0 copy-start
  55.3 0.6 copy-done
  55.9 0.0 copy-start.1
  55.9 0.6 copy-done.1
  56.5 0.0 copy-start.2
  56.5 0.6 copy-done.2
  57.1 7.3 %shard_map.77 = (f32[16,1536]{1,0:T(8,128)}, f32[16,1536]{1,0:T(8,128)}, f32[16,16]{1,0:T(8,128)}) custom-call(f32[16,1536]{1,0:T(8,128)} %copy-done, f32[16,1536]{1,0:T(8,128)} %copy-done.1, f32[16,16]{1,0:T(8,128)} %copy-done.2), custom_call_target="tpu_custom_call" | custom-call | tf_op jit(solution)/shard_map/pallas_call | solution.py:546
Async XLA Ops:
  55.2 0.6 copy-start
  55.9 0.6 copy-start.1
  56.5 0.6 copy-start.2

commit v7 on v6

--- a/solution.py
+++ b/solution.py
@@ -70,6 +70,7 @@
     ) = refs[:30]
     rounds = [refs[30:45], refs[45:60]]
     (ir_s, ir_r, ic_s, ic_r, c1_s, c1_r, c2_s, c2_r, g1_s, g1_r, g2_s, g2_r) = refs[60:72]
+    first_1, first_2, f1_s, f1_r, f2_s, f2_r = refs[72:78]
     nv = vec.shape[0]
     slots = raw.shape[0]
     row = lax.axis_index("row")
@@ -273,7 +274,7 @@
             lax.fori_loop(i * per, (i + 1) * per, step, 0)
 
     def multiply(line, blocks, pick, n, out, dot):
-        width = 16 if slots % 16 == 0 else 1
+        width = 24 if slots % 24 == 0 else 1
 
         def step(g, carry):
             for u in range(width):
@@ -367,18 +368,46 @@
                     own[self.which + 1, b, h * part_nv:(h + 1) * part_nv] = total
                 after_half(h)
 
+    def total_of(ref, n):
+        total = ref[0]
+        for i in range(1, n):
+            total = total + ref[i]
+        return total
+
+    first_row = Exchange("row", lambda p: first_1.at[row], lambda i: first_1.at[i], f1_s, f1_r)
+    first_col = Exchange("col", lambda p: first_2.at[col], lambda i: first_2.at[i], f2_s, f2_r)
+    exchanges.extend([first_row, first_col])
+
     def own_correlation():
         total = jnp.zeros((nv, nv), F32)
         for b in range(segb):
             total = total + dot_nt(own[0, b], own[0, b], EXACT)
-        small[0] = jnp.zeros_like(small[0])
-        small[0, 0:nv, 0:nv] = total
+        first_1[row] = pack_square(total)
+        first_row.start()
+        split_tiles()
+
+    def correlation_on():
+        first_row.wait_recv()
+        first_2[col] = total_of(first_1, n_row)
+        first_col.start()
+
+    def invert():
+        first_col.wait_recv()
+        correlation = unpack_square(total_of(first_2, n_col), nv)
+        line = iota((nv, 2 * nv), 0)
+        lane = iota((nv, 2 * nv), 1)
+        second = one_hot(lane == line + nv)
+        m = dot_nn(correlation, one_hot(lane == line), EXACT) + second
+        for i in range(nv):
+            pivot_row = m[i:i + 1, :] / m[i:i + 1, i:i + 1]
+            m = jnp.where(line == i, pivot_row, m - m[:, i:i + 1] * pivot_row)
+        small[0, 0:nv, 0:nv] = dot_nt(second, m, EXACT)
 
     nothing = lambda *unused: None
     one, two = Round(0), Round(1)
     for h in range(2):
         one.pack(h)
-    one.apply(split_tiles, nothing, own_correlation, nothing, nothing, two.pack)
+    one.apply(own_correlation, correlation_on, nothing, nothing, invert, two.pack)
 
     corr_row = Exchange("row", lambda p: corr_1.at[row], lambda i: corr_1.at[i], c1_s, c1_r)
     corr_col = Exchange("col", lambda p: corr_2.at[col], lambda i: corr_2.at[i], c2_s, c2_r)
@@ -386,12 +415,6 @@
     gram_col = Exchange("col", lambda p: gram_2.at[col], lambda i: gram_2.at[i], g2_s, g2_r)
     exchanges.extend([corr_row, corr_col, gram_row, gram_col])
 
-    def total_of(ref, n):
-        total = ref[0]
-        for i in range(1, n):
-            total = total + ref[i]
-        return total
-
     def fold(total, n):
         return total[0:n, 0:n] + total[0:n, n:2 * n] + total[n:2 * n, 0:n] + total[n:2 * n, n:2 * n]
 
@@ -400,9 +423,7 @@
         for b in range(segb):
             both = jnp.concatenate(split(jnp.concatenate([own[0, b], own[1, b]], axis=0)), axis=0)
             total = total + dot_nt(both, both)
-        total = fold(total, 2 * nv)
-        head = (iota((2 * nv, 2 * nv), 0) < nv) & (iota((2 * nv, 2 * nv), 1) < nv)
-        corr_1[row] = pack_square(jnp.where(head, small[0, :, 0:2 * nv], total))
+        corr_1[row] = pack_square(fold(total, 2 * nv))
         corr_row.start()
 
     def correlate_on():
@@ -433,15 +454,8 @@
         gram_col.start()
         corr_col.wait_recv()
         sums = unpack_square(total_of(corr_2, n_col), 2 * nv)
-        lanes = 2 * nv
-        m = sums[0:nv]
-        line = lax.broadcasted_iota(jnp.int32, (nv, lanes), 0)
-        lane = lax.broadcasted_iota(jnp.int32, (nv, lanes), 1)
-        for i in range(nv):
-            pivot_row = m[i:i + 1, :] / m[i:i + 1, i:i + 1]
-            m = jnp.where(line == i, pivot_row, m - m[:, i:i + 1] * pivot_row)
-        second = jnp.where(lane == line + nv, 1.0, 0.0).astype(F32)
-        coeffs_t = dot_nt(second, m, EXACT)
+        second = one_hot(iota((nv, 2 * nv), 1) == iota((nv, 2 * nv), 0) + nv)
+        coeffs_t = dot_nn(sums[nv:2 * nv, 0:nv], small[0, 0:nv, 0:nv], EXACT)
         proj = dot_nt(sums[0:nv], second, EXACT)
         squares = dot_nt(sums[nv:2 * nv], second, EXACT)
         for b in range(segb):
@@ -462,14 +476,6 @@
     out_copy.wait()
     for e in exchanges:
         e.wait_send()
-
-
-def hand_on(*refs):
-    copies = [pltpu.make_async_copy(refs[i], refs[3 + i], refs[6].at[i]) for i in range(3)]
-    for c in copies:
-        c.start()
-    for c in copies:
-        c.wait()
 
 
 def per_device(n_row, n_col, vectors, tiles, tile_rows, tile_cols, counts):
@@ -527,9 +533,12 @@
         dma((n_col,)), dma((n_col,)), dma((n_row,)), dma((n_row,)),
         dma((n_row,)), dma((n_row,)), dma((n_col,)), dma((n_col,)),
         dma((n_row,)), dma((n_row,)), dma((n_col,)), dma((n_col,)),
+        pltpu.VMEM((n_row, nv * nv // 128, 128), F32),
+        pltpu.VMEM((n_col, nv * nv // 128, 128), F32),
+        dma((n_row,)), dma((n_row,)), dma((n_col,)), dma((n_col,)),
     ]
     order = width * n_row * n_col
-    results = pl.pallas_call(
+    return pl.pallas_call(
         functools.partial(main_kernel, n_row, n_col, segb, order),
         out_shape=(
             jax.ShapeDtypeStruct((nv, width), F32),
@@ -543,13 +552,6 @@
             collective_id=0, has_side_effects=True, vmem_limit_bytes=52 * 2**20
         ),
     )(in_hbm(tile_rows), in_hbm(tile_cols), counts, in_hbm(vectors), tiles)
-    return pl.pallas_call(
-        hand_on,
-        out_shape=tuple(jax.ShapeDtypeStruct(x.shape, x.dtype) for x in results),
-        in_specs=[anywhere] * 3,
-        out_specs=(hbm,) * 3,
-        scratch_shapes=[dma((3,))],
-    )(*results)
 
 
 def solution(mesh):

time: 64.6 us -> 58 us (0.90)
  Pallas kernels: 61.3 us -> 54.7 us
    pallas_call x1 -> x0, Pallas kernels: 7.33 us -> none  [per_device(): pl.pallas_call(hand_on, out_shape=tuple((jax.ShapeDtypeStruct(x.shape, x....]
    pallas_call x1, Pallas kernels: 54 us -> 54.7 us  [per_device(): pl.pallas_call(functools.partial(main_kernel, n_row, n_col, segb, order),...]
    unnamed x6 -> x3, local copies, waits for them, and re-layouts: 1.84 us -> 1.88 us
where the time goes in v7:
time: 58 us; the launch traced here: 57.9 us
  Pallas kernels  54.7 us (94%)
  local copies, waits for them, and re-layouts  1.88 us (3%)
  between operations  1.29 us (2%)
    pallas_call x1, Pallas kernels, per_device(): pl.pallas_call(functools.partial(main_kernel, n_row, n_col, segb, order),...  54.7 us
    unnamed x3, local copies, waits for them, and re-layouts  1.88 us

profile of v7, /device:TPU:0, one launch (start us, length us, event | category | flops | bytes accessed | tf_op | source)
XLA Modules:
  0.0 57.9 jit_solution(15553635737837773142)
XLA Ops:
  1.3 54.7 %shard_map.76 = (f32[16,1536]{1,0:T(8,128)S(1)}, f32[16,1536]{1,0:T(8,128)S(1)}, f32[16,16]{1,0:T(8,128)S(1)}) custom-call(s32[1,1,48]{2,1,0:T(1,128)} %refs_0_.1, s32[1,1,48]{2,1,0:T(1,128)} %refs_1_.1, s32[1,1]{1,0:T(1,128)S(6)} %copy.11.refs_2_, f32[16,1536]{1,0:T(8,128)} %refs_3_.1, f32[1,1,48,256,256]{4,3,2,1,0:T(8,128)} %refs_4_.1), custom_call_target="tpu_custom_call" | custom-call | tf_op jit(solution)/shard_map/pallas_call | solution.py:541
  56.0 0.6 %copy.12 = f32[16,1536]{1,0:T(8,128)} copy(f32[16,1536]{1,0:T(8,128)S(1)} %get-tuple-element.6) | data formatting | bytes 196608
  56.6 0.6 %copy.13 = f32[16,1536]{1,0:T(8,128)} copy(f32[16,1536]{1,0:T(8,128)S(1)} %get-tuple-element.7) | data formatting | bytes 196608
  57.3 0.6 %copy.14 = f32[16,16]{1,0:T(8,128)} copy(f32[16,16]{1,0:T(8,128)S(1)} %get-tuple-element.8) | data formatting | bytes 2048

commit v8 on v6

--- a/solution.py
+++ b/solution.py
@@ -462,14 +462,6 @@
     out_copy.wait()
     for e in exchanges:
         e.wait_send()
-
-
-def hand_on(*refs):
-    copies = [pltpu.make_async_copy(refs[i], refs[3 + i], refs[6].at[i]) for i in range(3)]
-    for c in copies:
-        c.start()
-    for c in copies:
-        c.wait()
 
 
 def per_device(n_row, n_col, vectors, tiles, tile_rows, tile_cols, counts):
@@ -529,7 +521,7 @@
         dma((n_row,)), dma((n_row,)), dma((n_col,)), dma((n_col,)),
     ]
     order = width * n_row * n_col
-    results = pl.pallas_call(
+    return pl.pallas_call(
         functools.partial(main_kernel, n_row, n_col, segb, order),
         out_shape=(
             jax.ShapeDtypeStruct((nv, width), F32),
@@ -543,13 +535,6 @@
             collective_id=0, has_side_effects=True, vmem_limit_bytes=52 * 2**20
         ),
     )(in_hbm(tile_rows), in_hbm(tile_cols), counts, in_hbm(vectors), tiles)
-    return pl.pallas_call(
-        hand_on,
-        out_shape=tuple(jax.ShapeDtypeStruct(x.shape, x.dtype) for x in results),
-        in_specs=[anywhere] * 3,
-        out_specs=(hbm,) * 3,
-        scratch_shapes=[dma((3,))],
-    )(*results)
 
 
 def solution(mesh):

time: 64.6 us -> 57.3 us (0.89)
  Pallas kernels: 61.3 us -> 54 us
    pallas_call x1 -> x0, Pallas kernels: 7.33 us -> none  [per_device(): pl.pallas_call(hand_on, out_shape=tuple((jax.ShapeDtypeStruct(x.shape, x....]
    unnamed x6 -> x3, local copies, waits for them, and re-layouts: 1.84 us -> 1.88 us
where the time goes in v8:
time: 57.3 us; the launch traced here: 57.1 us
  Pallas kernels  54 us (94%)
  local copies, waits for them, and re-layouts  1.88 us (3%)
  between operations  1.29 us (2%)
    pallas_call x1, Pallas kernels, per_device(): pl.pallas_call(functools.partial(main_kernel, n_row, n_col, segb, order),...  54 us
    unnamed x3, local copies, waits for them, and re-layouts  1.88 us

profile of v8, /device:TPU:0, one launch (start us, length us, event | category | flops | bytes accessed | tf_op | source)
XLA Modules:
  0.0 57.1 jit_solution(18102278099648250413)
XLA Ops:
  1.3 54.0 %shard_map.76 = (f32[16,1536]{1,0:T(8,128)S(1)}, f32[16,1536]{1,0:T(8,128)S(1)}, f32[16,16]{1,0:T(8,128)S(1)}) custom-call(s32[1,1,48]{2,1,0:T(1,128)} %refs_0_.1, s32[1,1,48]{2,1,0:T(1,128)} %refs_1_.1, s32[1,1]{1,0:T(1,128)S(6)} %copy.11.refs_2_, f32[16,1536]{1,0:T(8,128)} %refs_3_.1, f32[1,1,48,256,256]{4,3,2,1,0:T(8,128)} %refs_4_.1), custom_call_target="tpu_custom_call" | custom-call | tf_op jit(solution)/shard_map/pallas_call | solution.py:524
  55.2 0.6 %copy.12 = f32[16,1536]{1,0:T(8,128)} copy(f32[16,1536]{1,0:T(8,128)S(1)} %get-tuple-element.6) | data formatting | bytes 196608
  55.9 0.6 %copy.13 = f32[16,1536]{1,0:T(8,128)} copy(f32[16,1536]{1,0:T(8,128)S(1)} %get-tuple-element.7) | data formatting | bytes 196608
  56.5 0.6 %copy.14 = f32[16,16]{1,0:T(8,128)} copy(f32[16,16]{1,0:T(8,128)S(1)} %get-tuple-element.8) | data formatting | bytes 2048
